TPU v7x, 256 devices: a whole 4x4x8 slice. The times are simulated.
256 devices in a mesh: ra: 32 (over x, z_hi, y), dec: 8 (over z_lo, core).
Axes of the slice: x: 4, y: 4, z: 8 (z_hi: 2, z_lo: 4; z = z_hi * 4 + z_lo), core: 2. Of those that a mesh axis runs over, the one named last changes fastest.
Arguments:
- cube: float32 [32, 512, 4096], P('ra', 'dec'), may hold values from -40 to 40, as said below
Outputs:
- snr: float32 [3, 2, 32, 512, 4096], P(None, None, None, 'dec', 'ra')
Inputs may be any that keep to these rules, and one draw needn't show every extreme that they name: A float cube.
All inputs are finite; a program needn't handle non-finite values.
Results may differ from a plain program's by a relative error of at most 0.00025.
Values sent between devices are 32-bit elements; how exact they have to be, the bound alone decides.
No kernel may reach another device: no remote copies, remote signals or barrier semaphores. Data moves between devices by JAX's collectives and lax.ppermute only.
A program may use at most 64 MiB of HBM per device.

v0:
```python
import functools

import jax
import jax.numpy as jnp
import ml_dtypes
import numpy as np
from jax import lax
from jax.experimental import pallas as pl
from jax.experimental.pallas import tpu as pltpu
from jax.sharding import PartitionSpec as P

sigma_values = (1, 2, 4)
boxcar_widths = (3, 7)
epsilon = 1e-06

LANES = 128
ROWS = 64
EDGE = 16
OUT = 40
HALF = 40
CHUNK = 2 * HALF
edge_rows = tuple(range(0, EDGE)) + tuple(range(ROWS - EDGE, ROWS))
middle_rows = tuple(range(EDGE, ROWS - EDGE))
tile_rows = edge_rows + middle_rows
halo_rows = tuple(range(-EDGE, 0)) + tuple(range(ROWS, ROWS + EDGE))
inner_out = middle_rows + (EDGE - 1, ROWS - EDGE)
outer_out = edge_rows + (-1, EDGE, ROWS - EDGE - 1, ROWS)
inner_runs = ((0, 32, 32, 33),)
outer_runs = ((0, 16, 32, 33), (16, 16, 34, 35))
beside_cols = np.array(tuple(range(LANES, LANES + 16)) + tuple(range(-16, 0)))


def taps(distance, sigma):
    reach = 3 * sigma
    lags = np.arange(-reach, reach + 1, dtype=np.float64)
    weight_sum = np.sum(np.exp(-lags * lags / (2.0 * sigma * sigma)))
    value = np.exp(-(distance.astype(np.float64) ** 2) / (2.0 * sigma * sigma)) / weight_sum
    return np.where(np.abs(distance) <= reach, value, 0.0).astype(np.float32)


def halves(value):
    high = value.astype(ml_dtypes.bfloat16)
    low = (value - high.astype(np.float32)).astype(ml_dtypes.bfloat16)
    return high, low


def ra_weights():
    def band(cols):
        weights = np.zeros((len(cols), 4 * LANES), np.float32)
        for s, sigma in enumerate(sigma_values):
            weights[:, s * LANES : (s + 1) * LANES] = taps(
                cols[:, None] - np.arange(LANES)[None, :], sigma
            )
            for side, col in enumerate((-1, LANES)):
                weights[:, 3 * LANES + 32 * s + side] = taps(cols - col, sigma)
        return halves(weights)

    high, low = band(np.arange(LANES))
    beside_high, beside_low = band(beside_cols)
    nothing = np.zeros_like(beside_high)
    parts = [high, high, low, beside_high, beside_high, beside_low, nothing]
    return np.concatenate(parts, axis=0)


def dec_weights(out_rows, in_rows):
    result = np.zeros((3, 2 * OUT, 2 * len(in_rows)), ml_dtypes.bfloat16)
    for s, sigma in enumerate(sigma_values):
        weights = taps(np.array(in_rows)[None, :] - np.array(out_rows)[:, None], sigma)
        high, low = halves(weights)
        result[s, : len(out_rows), : len(in_rows)] = high
        result[s, : len(out_rows), len(in_rows) :] = high
        result[s, OUT : OUT + len(out_rows), : len(in_rows)] = low
    return result


def edge_weights(channels):
    half = channels // 2
    lane = np.arange(2 * LANES)
    tile, within = lane // LANES, lane % LANES
    sigma, slot = within // 32, within % 32
    channel, side = tile * half + slot // 2, slot % 2
    used = (sigma < 3) & (slot < 2 * half)
    same = used[:, None] & used[None, :] & (sigma[:, None] == sigma[None, :])
    same &= side[:, None] == side[None, :]
    boxcars = [
        same & (np.abs(channel[:, None] - channel[None, :]) <= width // 2)
        for width in boxcar_widths
    ]
    gathers = np.zeros((3, 2 * LANES, LANES), bool)
    for s in range(3):
        gathers[s, :, 0] = used & (sigma == s) & (side == 0)
        gathers[s, :, LANES - 1] = used & (sigma == s) & (side == 1)
    return (
        np.stack(boxcars).astype(ml_dtypes.bfloat16),
        gathers.astype(ml_dtypes.bfloat16),
    )


def lane_index(shape):
    return lax.broadcasted_iota(jnp.int32, shape, len(shape) - 1)


def split(value):
    high = value.astype(jnp.bfloat16)
    low = (value - high.astype(jnp.float32)).astype(jnp.bfloat16)
    return high, low


def dot(a, b):
    return jnp.dot(a, b, preferred_element_type=jnp.float32)


def pack_rows(block, out_ref, tile, at):
    lane = lane_index((8, LANES))
    here, right, left = block
    packed = jnp.zeros((8, LANES), jnp.float32)
    for group in range(4):
        out_ref[tile, at + 8 * group : at + 8 * group + 8, :] = here(group)
        first, first_at = right(group)
        last, last_at = left(group)
        first = turn(first, 32 * group - first_at)
        last = turn(last, 32 * group + 16 - last_at)
        lanes = lane - 32 * group
        packed = jnp.where((lanes >= 0) & (lanes < 16), first, packed)
        packed = jnp.where((lanes >= 16) & (lanes < 32), last, packed)
    out_ref[tile, at + 32 : at + HALF, :] = packed


def turn(value, lanes):
    lanes = lanes % LANES
    return pltpu.roll(value, lanes, 1) if lanes else value


def far_half():
    return 1 - (lax.axis_index("ra") // 4) % 2


def rows_copies(cube_ref, rows, held, sems):
    copies = []
    for k, at in enumerate(range(0, len(rows), 16)):
        source = cube_ref.at[0, pl.ds(rows[at], 16), :]
        copies.append(pltpu.make_async_copy(source, held.at[pl.ds(at, 16), :], sems.at[k]))
    for copy in copies:
        copy.start()
    return copies


def column_kernel(tiles, cube_ref, far_ref, near_ref, held, sems):
    copies = rows_copies(cube_ref, edge_rows, held, sems)
    far = far_half()
    lane = lane_index((8, LANES))
    wide = tiles // 8

    def columns(tile, at):
        return held[at : at + 8, pl.ds(pl.multiple_of(tile * LANES, LANES), LANES)]

    for group in range(4):
        at = 8 * group
        if group % 2 == 0:
            copies[group // 2].wait()
        for half_z, out_ref in ((far, far_ref), (1 - far, near_ref)):
            beside = jnp.zeros((8, LANES), jnp.float32)
            for x in range(wide):
                first = 8 * x + 4 * half_z
                for y in range(4):
                    out_ref[4 * x + y, at : at + 8, :] = columns(first + y, at)
                right = turn(columns(jnp.minimum(first + 4, tiles - 1), at), 32 * x)
                left = turn(columns(jnp.maximum(first - 1, 0), at), 32 * x + 32)
                right = jnp.where(first + 4 < tiles, right, 0.0)
                left = jnp.where(first > 0, left, 0.0)
                lanes = lane - 32 * x
                beside = jnp.where((lanes >= 0) & (lanes < 16), right, beside)
                beside = jnp.where((lanes >= 16) & (lanes < 32), left, beside)
            out_ref[4 * wide, at : at + 8, :] = beside


def pack_cube(tiles, held, half_z, out_ref, at):
    def columns(tile, group):
        inside = (tile >= 0) & (tile < tiles)
        tile = jnp.clip(tile, 0, tiles - 1)
        lanes = pl.ds(pl.multiple_of(tile * LANES, LANES), LANES)
        return inside, held[8 * group : 8 * group + 8, lanes]

    for x in range(tiles // 8):
        for y in range(4):
            tile = 8 * x + 4 * half_z + y

            def here(group):
                return columns(tile, group)[1]

            def right(group):
                inside, value = columns(tile + 1, group)
                return (jnp.where(inside, value, 0.0) if y == 3 else value), 0

            def left(group):
                inside, value = columns(tile - 1, group)
                return (jnp.where(inside, value, 0.0) if y == 0 else value), LANES - 16

            pack_rows((here, right, left), out_ref, 4 * x + y, at)


def middle_kernel(tiles, cube_ref, out_ref, held, sems):
    for copy in rows_copies(cube_ref, middle_rows, held, sems):
        copy.wait()
    far = far_half()
    pack_cube(tiles, held, far, out_ref, 0)
    pack_cube(tiles, held, 1 - far, out_ref, HALF)


def edge_rows_kernel(after_ref, far_ref, near_ref, out_ref):
    del after_ref
    wide = out_ref.shape[0] // 4
    for start, ref in ((0, far_ref), (HALF, near_ref)):
        for x in range(wide):
            for y in range(4):
                tile = 4 * x + y

                def here(group):
                    return ref[tile, 8 * group : 8 * group + 8, :]

                def right(group):
                    if y < 3:
                        return ref[tile + 1, 8 * group : 8 * group + 8, :], 0
                    return ref[4 * wide, 8 * group : 8 * group + 8, :], 32 * x

                def left(group):
                    if y > 0:
                        return ref[tile - 1, 8 * group : 8 * group + 8, :], LANES - 16
                    return ref[4 * wide, 8 * group : 8 * group + 8, :], 32 * x + 16

                pack_rows((here, right, left), out_ref, tile, start)


def edge_kernel(edge_ref, top_ref, bottom_ref):
    count = edge_ref.shape[0]
    channels = 2 * count
    lane = lane_index((8, LANES))
    for part, start in enumerate((HALF, 0)):
        for i in range(count):
            at = (part * count + i) * EDGE
            top_ref[at : at + EDGE, :] = edge_ref[i, start : start + EDGE, :]
            bottom_ref[at : at + EDGE, :] = edge_ref[i, start + EDGE : start + 2 * EDGE, :]
        for pair in range(count // 2):
            at = channels * EDGE + 8 * (part * count // 2 + pair)
            first = edge_ref[2 * pair, start + 32 : start + HALF, :]
            second = edge_ref[2 * pair + 1, start + 32 : start + HALF, :]
            top_ref[at : at + 8, :] = jnp.where(lane < 64, first, pltpu.roll(second, 64, 1))
            bottom_ref[at : at + 8, :] = jnp.where(lane < 64, pltpu.roll(first, 64, 1), second)


def put_rows(source, at, main, packed, places):
    lane = lane_index((8, LANES))
    high, low = split(main)
    beside = []
    for value, place in zip(packed, places):
        value_high = value.astype(jnp.bfloat16).astype(jnp.float32)
        value_low = value - value_high
        mix = jnp.where(lane < 64, turn(value_low, 32 - place), turn(value_high, 64 - place))
        mix = jnp.where(lane < 32, turn(value_high, -place), mix)
        beside.append(jnp.where(lane < 96, mix, 0.0))
    source[at : at + 16, :LANES] = low
    source[at : at + 16, LANES : 2 * LANES] = high
    source[at : at + 16, 2 * LANES :] = jnp.concatenate(beside, axis=0).astype(jnp.bfloat16)


def smooth_ra(source, weights_ref, rows, pairs, channels_at, done, edges):
    operand = jnp.concatenate([source[:, : 2 * LANES], source[:, LANES:]], axis=1)
    along = dot(operand, weights_ref[...])
    half = done.shape[1]
    for j, (pair, c) in enumerate(zip(pairs, channels_at)):
        block = along[j * rows : (j + 1) * rows]
        lanes = slice((j % 2) * LANES, (j % 2 + 1) * LANES)
        for s in range(3):
            high, low = split(block[:, s * LANES : (s + 1) * LANES])
            done[s, pair, :rows, lanes] = high
            done[s, pair, rows:, lanes] = low
        tile, slot = c // half, c % half
        edges[tile] = edges[tile] + pltpu.roll(block[:, 3 * LANES :], 2 * slot, 1)


def smooth_dec(parts, s, pair):
    both = sum(dot(weights[s], done[s, pair]) for weights, done in parts)
    return both[:OUT] + both[OUT:]


def beside_squares(parts, box_ref, gather_ref):
    which = lane_index((OUT, 2 * LANES)) % LANES // 32
    smoothed = jnp.zeros((OUT, 2 * LANES), jnp.float32)
    parts = [
        (weights, jnp.concatenate(split(jnp.concatenate([edges[0], edges[1]], axis=1)), axis=0))
        for weights, edges in parts
    ]
    for s in range(3):
        both = sum(dot(weights[s], value) for weights, value in parts)
        smoothed = jnp.where(which == s, both[:OUT] + both[OUT:], smoothed)
    smoothed = split(smoothed)
    result = []
    for b in range(2):
        summed = dot(smoothed[0], box_ref[b]) + dot(smoothed[1], box_ref[b])
        square = split(summed * summed)
        result.append(
            [dot(square[0], gather_ref[s]) + dot(square[1], gather_ref[s]) for s in range(3)]
        )
    return result


def snr_rows(parts, beside, outside, runs, targets, smooth, result, framed, sems):
    channels = result.shape[1]
    ra_at, ra_n = lax.axis_index("ra"), lax.axis_size("ra")
    lane = lane_index((OUT, LANES))
    row = lax.broadcasted_iota(jnp.int32, (OUT, LANES), 0)
    gone = row < 0
    for at, condition in outside:
        gone = gone | ((row == at) & condition)
    no_side = ((lane == 0) & (ra_at == 0)) | ((lane == LANES - 1) & (ra_at == ra_n - 1))
    rows = sum(run[1] for run in runs)
    copies = []
    for s in range(3):

        def smooth_pair(pair, carry):
            both = smooth_dec(parts, s, pair)
            smooth[3 + 2 * pair] = both[:, :LANES]
            smooth[4 + 2 * pair] = both[:, LANES:]
            return carry

        for k in range(3):
            smooth[k] = jnp.zeros((OUT, LANES), jnp.float32)
            smooth[3 + channels + k] = jnp.zeros((OUT, LANES), jnp.float32)
        lax.fori_loop(0, channels // 2, smooth_pair, 0, unroll=4)

        squares = [[], []]
        for at in range(0, OUT, 8):
            planes = [smooth[k, at : at + 8, :] for k in range(channels + 6)]
            triples = [planes[k] + planes[k + 1] + planes[k + 2] for k in range(channels + 4)]
            totals = [[None, None], [None, None]]
            for c in range(channels):
                wide = triples[c] + triples[c + 3] + planes[c + 6]
                for b, value in enumerate((triples[c + 2], wide)):
                    if at < rows:
                        result[2 * s + b, c, at : at + 8, :] = value
                    square = value * value
                    total = totals[b][c % 2]
                    totals[b][c % 2] = square if total is None else total + square
            for b in range(2):
                squares[b].append(totals[b][0] + totals[b][1])
        for b, width in enumerate(boxcar_widths):
            square = jnp.where(gone, 0.0, jnp.concatenate(squares[b], axis=0))
            across = square + jnp.where(no_side | gone, 0.0, beside[b][s])
            across = across + jnp.where(lane == 0, 0.0, pltpu.roll(square, 1, 1))
            across = across + jnp.where(lane == LANES - 1, 0.0, pltpu.roll(square, LANES - 1, 1))
            boxed = []
            at = 0
            for first, length, before, after in runs:
                at = at + 8
                framed[at : at + length] = across[first : first + length]
                framed[at - 1 : at] = across[before : before + 1]
                framed[at + length : at + length + 1] = across[after : after + 1]
                boxed.append(
                    framed[at - 1 : at - 1 + length]
                    + framed[at : at + length]
                    + framed[at + 1 : at + 1 + length]
                )
                at = at + length + 8
            boxed = jnp.concatenate(boxed, axis=0) if len(boxed) > 1 else boxed[0]
            scale = 1.0 / jnp.sqrt(boxed / (9.0 * channels) + width * width * epsilon)

            def normalize(c, carry):
                result[2 * s + b, c] = result[2 * s + b, c] * scale
                return carry

            lax.fori_loop(0, channels, normalize, 0, unroll=8)
            for k, (first, length, _, _) in enumerate(runs):
                copy = pltpu.make_async_copy(
                    result.at[2 * s + b, :, pl.ds(first, length), :],
                    targets(s, b)[k],
                    sems.at[len(runs) * (2 * s + b) + k],
                )
                copy.start()
                copies.append(copy)
    for copy in copies:
        copy.wait()


def inner_kernel(
    edge_ref, middle_ref, far_middle_ref, ra_ref, dec_ref, box_ref, gather_ref,
    out_ref, done_ref, edges_ref,
    source, smooth, result, framed, sems,
    *, batch,
):
    channels = 2 * edge_ref.shape[0]
    near = (lax.axis_index("ra") // 4) % 2
    edges_ref[...] = jnp.zeros_like(edges_ref)
    halves_of = ((edge_ref, HALF), (middle_ref, HALF)), ((edge_ref, 0), (far_middle_ref, 0))
    for part, parts in enumerate(halves_of):
        half_z = near if part == 0 else 1 - near
        for step in range(channels // 2 // batch):
            pairs, channels_at = [], []
            for j in range(batch):
                i = step * batch + j
                for half, (ref, at) in enumerate(parts):
                    packed = ref[i, at + 32 : at + HALF, :]
                    for k in range(2):
                        main = ref[i, at + 16 * k : at + 16 * k + 16, :]
                        put_rows(
                            source.at[part], j * ROWS + 32 * half + 16 * k, main,
                            (packed, packed), (64 * k, 64 * k + 32),
                        )
                pairs.append(4 * (i // 4) + 2 * half_z + (i % 4) // 2)
                channels_at.append(8 * (i // 4) + 4 * half_z + i % 4)
            smooth_ra(source.at[part], ra_ref, ROWS, pairs, channels_at, done_ref, edges_ref)
    beside = beside_squares([(dec_ref, edges_ref)], box_ref, gather_ref)

    def targets(s, b):
        return [out_ref.at[s, b, :, pl.ds(EDGE, ROWS - 2 * EDGE), :]]

    snr_rows(
        [(dec_ref, done_ref)], beside, (), inner_runs, targets, smooth, result, framed, sems
    )


def outer_kernel(
    held_ref, above_ref, below_ref, done_ref, edges_ref,
    ra_ref, dec_ref, dec_halo_ref, box_ref, gather_ref,
    out_ref,
    source, halo_done, halo_edges, smooth, result, framed, sems,
    *, batch,
):
    del held_ref
    channels = 2 * done_ref.shape[1]
    near = (lax.axis_index("ra") // 4) % 2
    dec_at, dec_n = lax.axis_index("dec"), lax.axis_size("dec")
    halo_edges[...] = jnp.zeros_like(halo_edges)
    for step in range(channels // batch):
        pairs, channels_at = [], []
        for j in range(batch):
            at = step * batch + j
            part, i = at // (channels // 2), at % (channels // 2)
            for k, ref in enumerate((above_ref, below_ref)):
                row = channels * EDGE + 8 * (at // 2)
                packed = ref[row : row + 8, :]
                lanes = 64 * (at % 2)
                put_rows(
                    source.at[step % 2], 2 * EDGE * j + EDGE * k, ref[at * EDGE : (at + 1) * EDGE, :],
                    (packed, packed), (lanes, lanes + 32),
                )
            half_z = near if part == 0 else 1 - near
            pairs.append(4 * (i // 4) + 2 * half_z + (i % 4) // 2)
            channels_at.append(8 * (i // 4) + 4 * half_z + i % 4)
        smooth_ra(
            source.at[step % 2], ra_ref, 2 * EDGE, pairs, channels_at, halo_done, halo_edges
        )
    parts = [(dec_ref, done_ref), (dec_halo_ref, halo_done)]
    beside = beside_squares(
        [(dec_ref, edges_ref), (dec_halo_ref, halo_edges)], box_ref, gather_ref
    )

    def targets(s, b):
        return [out_ref.at[s, b, :, pl.ds(at, EDGE), :] for at in (0, ROWS - EDGE)]

    outside = ((32, dec_at == 0), (35, dec_at == dec_n - 1))
    snr_rows(parts, beside, outside, outer_runs, targets, smooth, result, framed, sems)


def local(cube):
    tiles = channels = lax.axis_size("ra")
    vmem = pl.BlockSpec(memory_space=pltpu.VMEM)
    f32 = jnp.float32

    def call(kernel, shapes, operands, name, outside=(), scratch=()):
        return pl.pallas_call(
            kernel,
            out_shape=shapes,
            in_specs=[pl.BlockSpec(memory_space=pl.ANY)] * len(outside) + [vmem] * len(operands),
            out_specs=jax.tree.map(lambda _: vmem, shapes),
            scratch_shapes=scratch,
            compiler_params=pltpu.CompilerParams(vmem_limit_bytes=32 * 2**20),
            name=name,
        )(*outside, *operands)

    across = [(i, i ^ 4) for i in range(tiles)]
    groups = [[8 * x + 4 * z + y for x in range(tiles // 8) for y in range(4)] for z in range(2)]

    def regroup(chunks):
        return lax.all_to_all(
            chunks, "ra", split_axis=0, concat_axis=0, tiled=True, axis_index_groups=groups
        )

    part = jax.ShapeDtypeStruct((tiles // 2 + 1, 32, LANES), f32)
    chunk = jax.ShapeDtypeStruct((tiles // 2, CHUNK, LANES), f32)
    rows = [pltpu.VMEM((32, cube.shape[2]), f32), pltpu.SemaphoreType.DMA((2,))]
    columns = functools.partial(column_kernel, tiles)
    part, near_part = call(columns, (part, part), (), "columns", (cube,), rows)
    part = lax.ppermute(part, "ra", across)

    def regroup_middle(cube):
        chunks = call(functools.partial(middle_kernel, tiles), chunk, (), "middle", (cube,), rows)
        return regroup(chunks)

    def nothing(cube):
        return jnp.zeros(chunk.shape, f32)

    middle = lax.cond(lax.axis_index("ra") >= 0, regroup_middle, nothing, cube)
    far_middle = lax.ppermute(middle[:, :HALF], "ra", across)
    edge = call(edge_rows_kernel, chunk, (part, near_part), "edge_rows", (middle,))
    edge_chunk = regroup(edge)
    edge = jax.ShapeDtypeStruct((channels * (EDGE + 4), LANES), f32)
    top, bottom = call(edge_kernel, (edge, edge), (edge_chunk,), "edges")
    count = lax.axis_size("dec")
    down = [(i, i + 1) for i in range(count - 1)]
    up = [(i + 1, i) for i in range(count - 1)]
    above = lax.ppermute(bottom, "dec", down)
    below = lax.ppermute(top, "dec", up)
    box, gather = (jnp.asarray(value) for value in edge_weights(channels))
    along = jnp.asarray(ra_weights())
    anywhere = pl.BlockSpec(memory_space=pl.ANY)
    out = jax.ShapeDtypeStruct((3, 2, channels, ROWS, LANES), f32)
    batch = 8
    work = [
        pltpu.VMEM((channels + 6, OUT, LANES), f32),
        pltpu.VMEM((6, channels, 2 * EDGE, LANES), f32),
        pltpu.VMEM((ROWS + 16, LANES), f32),
    ]
    params = pltpu.CompilerParams(vmem_limit_bytes=32 * 2**20)
    held, done, edges = pl.pallas_call(
        functools.partial(inner_kernel, batch=batch),
        out_shape=(
            out,
            jax.ShapeDtypeStruct((3, channels // 2, 2 * ROWS, 2 * LANES), jnp.bfloat16),
            jax.ShapeDtypeStruct((2, ROWS, LANES), f32),
        ),
        in_specs=[vmem] * 7,
        out_specs=(anywhere, vmem, vmem),
        scratch_shapes=[pltpu.VMEM((2, batch * ROWS, 3 * LANES), jnp.bfloat16)]
        + work
        + [pltpu.SemaphoreType.DMA((6,))],
        compiler_params=params,
        cost_estimate=pl.CostEstimate(
            flops=2 * 10**9, bytes_accessed=8 * 2**20, transcendentals=0
        ),
        name="inner",
    )(
        edge_chunk, middle, far_middle, along,
        jnp.asarray(dec_weights(inner_out, tile_rows)), box, gather,
    )
    batch = 16
    return pl.pallas_call(
        functools.partial(outer_kernel, batch=batch),
        out_shape=out,
        in_specs=[anywhere] + [vmem] * 9,
        out_specs=anywhere,
        scratch_shapes=[
            pltpu.VMEM((2, batch * 2 * EDGE, 3 * LANES), jnp.bfloat16),
            pltpu.VMEM((3, channels // 2, 4 * EDGE, 2 * LANES), jnp.bfloat16),
            pltpu.VMEM((2, 2 * EDGE, LANES), f32),
        ]
        + work
        + [pltpu.SemaphoreType.DMA((12,))],
        input_output_aliases={0: 0},
        compiler_params=params,
        cost_estimate=pl.CostEstimate(
            flops=10**9, bytes_accessed=8 * 2**20, transcendentals=0
        ),
        name="outer",
    )(
        held, above, below, done, edges, along,
        jnp.asarray(dec_weights(outer_out, tile_rows)),
        jnp.asarray(dec_weights(outer_out, halo_rows)), box, gather,
    )


def solution(mesh):
    return jax.shard_map(
        local,
        mesh=mesh,
        in_specs=(P("ra", "dec", None),),
        out_specs=P(None, None, None, "dec", "ra"),
        check_vma=False,
    )
```

profile of v0, /device:TPU:1, one launch (start us, length us, event | category | flops | bytes accessed | tf_op | source)
XLA Modules:
  0.0 65.1 jit_solution(9361311294984466331)
XLA Ops:
  0.0 0.0 copy-start
  0.0 0.0 copy-start.2
  0.0 0.0 copy-start.1
  0.0 0.0 copy-start.5
  0.0 1.3 %columns.1 = (f32[17,32,128]{2,1,0:T(8,128)S(1)}, f32[17,32,128]{2,1,0:T(8,128)S(1)}) custom-call(f32[1,64,4096]{2,1,0:T(8,128)} %cube_ref.2), custom_call_target="tpu_custom_call" | custom-call | tf_op jit(solution)/shard_map/columns/pallas_call | solution.py:470
  1.3 7.8 %collective-permute-start = (f32[17,32,128]{2,1,0:T(8,128)S(1)}, f32[17,32,128]{2,1,0:T(8,128)S(1)}, u32[]{:S(2)}, u32[]{:S(2)}) collective-permute-start(f32[17,32,128]{2,1,0:T(8,128)S(1)} %get-tuple-element.16), channel_id=1, source_target_pairs={{0,32},{8,40},{16,48},{24,56},{32,0},{40,8},{48,16},{56,24},{64,96... | collective-permute-start | bytes 835592 | tf_op jit(solution)/shard_map/ppermute | solution.py:493
  9.2 18.9 %conditional.1 = (f32[16,80,128]{2,1,0:T(8,128)S(1)}) conditional(s32[]{:T(128)} %convert_element_type.3, () %tuple.11, f32[1,64,4096]{2,1,0:T(8,128)} %cube_ref.2), branch_computations={%region_0.0_spmd, %region_1.0_spmd} | conditional | bytes 1310728 | solution.py:502
  9.2 1.3 %middle.1 = f32[16,80,128]{2,1,0:T(8,128)S(1)} custom-call(f32[1,64,4096]{2,1,0:T(8,128)} %cube_ref.1), custom_call_target="tpu_custom_call" | custom-call | tf_op jit(solution)/shard_map/cond/branch_1_fun/middle/pallas_call | solution.py:470
  10.5 17.6 %all_to_all.9 = f32[16,80,128]{2,1,0:T(8,128)S(1)} all-to-all(f32[16,80,128]{2,1,0:T(8,128)S(1)} %middle.1), channel_id=1, replica_groups={{0,8,16,24,64,72,80,88,128,136,144,152,192,200,208,216},{32,40,48,56,96..., dimensions={0} | all-to-all | bytes 1310720 | tf_op jit(solution)/shard_map/cond/branch_1_fun/all_to_all | solution.py:484
  28.1 0.0 copy-start.3
  28.1 0.0 copy-start.4
  28.1 0.0 collective-permute-done.far_ref
  28.1 1.1 %edge_rows.1 = f32[16,80,128]{2,1,0:T(8,128)} custom-call(f32[16,80,128]{2,1,0:T(8,128)S(1)} %get-tuple-element.23.after_ref.middle_ref, f32[17,32,128]{2,1,0:T(8,128)S(1)} %collective-permute-done.far_ref, f32[17,32,128]{2,1,0:T(8,128)S(1)} %get-tuple-element.17.near_ref), custom_call_target="tpu_custom_call" | custom-call | tf_op jit(solution)/shard_map/edge_rows/pallas_call | solution.py:470
  29.2 3.9 %all-to-all-start.1 = ((f32[16,80,128]{2,1,0:T(8,128)}), f32[16,80,128]{2,1,0:T(8,128)S(1)}, u32[]{:S(2)}, u32[]{:S(2)}) async-start(f32[16,80,128]{2,1,0:T(8,128)} %edge_rows.1), calls=%async_computation.1 | async-start | bytes 1310720 | tf_op jit(solution)/shard_map/all_to_all | solution.py:484
  33.1 0.4 collective-permute-start.1
  33.5 9.7 %all-to-all-done.1.edge_ref = f32[16,80,128]{2,1,0:T(8,128)S(1)} async-done(((f32[16,80,128]{2,1,0:T(8,128)}), f32[16,80,128]{2,1,0:T(8,128)S(1)}, u32[]{:S(2)}, u32[]{:S(2)}) %all-to-all-start.1) | async-done | bytes 655392 | tf_op jit(solution)/shard_map/all_to_all | solution.py:484
  43.3 0.1 edges.1
  43.4 6.2 %collective-permute-start.2 = (f32[640,128]{1,0:T(8,128)S(1)}, f32[640,128]{1,0:T(8,128)S(1)}, u32[]{:S(2)}, u32[]{:S(2)}) collective-permute-start(f32[640,128]{1,0:T(8,128)S(1)} %get-tuple-element.19), channel_id=1, source_target_pairs={{0,1},{1,2},{2,3},{3,4},{4,5},{5,6},{6,7},{8,9},{9,10},{10,11},{11... | collective-permute-start | bytes 983048 | tf_op jit(solution)/shard_map/ppermute | solution.py:511
  49.6 1.9 %collective-permute-start.3 = (f32[640,128]{1,0:T(8,128)S(1)}, f32[640,128]{1,0:T(8,128)S(1)}, u32[]{:S(2)}, u32[]{:S(2)}) collective-permute-start(f32[640,128]{1,0:T(8,128)S(1)} %get-tuple-element.20), channel_id=1, source_target_pairs={{1,0},{2,1},{3,2},{4,3},{5,4},{6,5},{7,6},{9,8},{10,9},{11,10},{12... | collective-permute-start | bytes 983048 | tf_op jit(solution)/shard_map/ppermute | solution.py:512
  51.5 0.0 collective-permute-done.1.far_middle_ref
  51.5 0.0 copy-done
  51.5 0.0 copy-done.2
  51.5 0.0 copy-done.1
  51.5 0.0 copy-done.5
  51.6 6.8 %inner.1 = (f32[3,2,32,64,128]{4,3,2,1,0:T(8,128)}, bf16[3,16,128,256]{3,2,1,0:T(8,128)(2,1)S(1)}, f32[2,64,128]{2,1,0:T(8,128)S(1)}) custom-call(f32[16,80,128]{2,1,0:T(8,128)S(1)} %all-to-all-done.1.edge_ref, f32[16,80,128]{2,1,0:T(8,128)S(1)} %get-tuple-element.23.after_ref.middle_ref, f32[16,40,128]{2,1,0:T(8,128)S(1)} %collective-permute-done.1.far_middle_ref, ...), custom_call_target="tpu_custom_call" | custom-call | flops 2000000000 | bytes 8388608 | tf_op jit(solution)/shard_map/inner/pallas_call | solution.py:524
  58.4 0.0 collective-permute-done.2.above_ref
  58.4 0.0 collective-permute-done.3.below_ref
  58.4 0.0 copy-done.3
  58.4 0.0 copy-done.4
  58.4 6.7 %outer.1 = f32[3,2,32,64,128]{4,3,2,1,0:T(8,128)} custom-call(f32[3,2,32,64,128]{4,3,2,1,0:T(8,128)} %get-tuple-element.18.held_ref, f32[640,128]{1,0:T(8,128)S(1)} %collective-permute-done.2.above_ref, f32[640,128]{1,0:T(8,128)S(1)} %collective-permute-done.3.below_ref, ...), custom_call_target="tpu_custom_call", output_to_operand_aliasing={{}: (0, {})} | custom-call | flops 1000000000 | bytes 8388608 | tf_op jit(solution)/shard_map/outer/pallas_call | solution.py:546
  (1 shorter events, 0.0 us)
Async XLA Ops:
  0.0 51.5 %copy-start = (bf16[512,512]{1,0:T(8,128)(2,1)S(1)}, bf16[512,512]{1,0:T(8,128)(2,1)}, u32[]{:S(2)}) copy-start(bf16[512,512]{1,0:T(8,128)(2,1)} %constant.24.clone.ra_ref) | copy-start | bytes 1572868
  0.0 51.5 %copy-start.2 = (bf16[3,256,128]{2,1,0:T(8,128)(2,1)S(1)}, bf16[3,256,128]{2,1,0:T(8,128)(2,1)}, u32[]{:S(2)}) copy-start(bf16[3,256,128]{2,1,0:T(8,128)(2,1)} %constant.23.clone.gather_ref) | copy-start | bytes 589828
  0.0 51.5 %copy-start.1 = (bf16[2,256,256]{2,1,0:T(8,128)(2,1)S(1)}, bf16[2,256,256]{2,1,0:T(8,128)(2,1)}, u32[]{:S(2)}) copy-start(bf16[2,256,256]{2,1,0:T(8,128)(2,1)} %constant.22.clone.box_ref) | copy-start | bytes 786436
  0.0 51.5 %copy-start.5 = (bf16[3,80,128]{2,1,0:T(8,128)(2,1)S(1)}, bf16[3,80,128]{2,1,0:T(8,128)(2,1)}, u32[]{:S(2)}) copy-start(bf16[3,80,128]{2,1,0:T(8,128)(2,1)} %constant.25.clone.dec_ref) | copy-start | bytes 184324
  1.3 26.8 %collective-permute-start = (f32[17,32,128]{2,1,0:T(8,128)S(1)}, f32[17,32,128]{2,1,0:T(8,128)S(1)}, u32[]{:S(2)}, u32[]{:S(2)}) collective-permute-start(f32[17,32,128]{2,1,0:T(8,128)S(1)} %get-tuple-element.16), channel_id=1, source_target_pairs={{0,32},{8,40},{16,48},{24,56},{32,0},{40,8},{48,16},{56,24},{64,96... | collective-permute-start | bytes 835592 | tf_op jit(solution)/shard_map/ppermute | solution.py:493
  28.1 30.3 %copy-start.3 = (bf16[3,80,64]{2,1,0:T(8,128)(2,1)S(1)}, bf16[3,80,64]{2,1,0:T(8,128)(2,1)}, u32[]{:S(2)}) copy-start(bf16[3,80,64]{2,1,0:T(8,128)(2,1)} %constant.27.clone.dec_halo_ref) | copy-start | bytes 92164
  28.1 30.3 %copy-start.4 = (bf16[3,80,128]{2,1,0:T(8,128)(2,1)S(1)}, bf16[3,80,128]{2,1,0:T(8,128)(2,1)}, u32[]{:S(2)}) copy-start(bf16[3,80,128]{2,1,0:T(8,128)(2,1)} %constant.26.clone.dec_ref) | copy-start | bytes 184324
  29.2 14.1 %all-to-all-start.1 = ((f32[16,80,128]{2,1,0:T(8,128)}), f32[16,80,128]{2,1,0:T(8,128)S(1)}, u32[]{:S(2)}, u32[]{:S(2)}) async-start(f32[16,80,128]{2,1,0:T(8,128)} %edge_rows.1), calls=%async_computation.1 | async-start | bytes 1310720 | tf_op jit(solution)/shard_map/all_to_all | solution.py:484
  33.1 18.4 %collective-permute-start.1 = (f32[16,40,128]{2,1,0:T(8,128)S(1)}, f32[16,40,128]{2,1,0:T(8,128)S(1)}, u32[]{:S(2)}, u32[]{:S(2)}) collective-permute-start(f32[16,40,128]{2,1,0:T(8,128)S(1)} %slice.4), channel_id=1, source_target_pairs={{0,32},{8,40},{16,48},{24,56},{32,0},{40,8},{48,16},{56,24},{64,96... | collective-permute-start | bytes 983048 | tf_op jit(solution)/shard_map/ppermute | solution.py:503
  43.4 15.0 %collective-permute-start.2 = (f32[640,128]{1,0:T(8,128)S(1)}, f32[640,128]{1,0:T(8,128)S(1)}, u32[]{:S(2)}, u32[]{:S(2)}) collective-permute-start(f32[640,128]{1,0:T(8,128)S(1)} %get-tuple-element.19), channel_id=1, source_target_pairs={{0,1},{1,2},{2,3},{3,4},{4,5},{5,6},{6,7},{8,9},{9,10},{10,11},{11... | collective-permute-start | bytes 983048 | tf_op jit(solution)/shard_map/ppermute | solution.py:511
  49.6 8.8 %collective-permute-start.3 = (f32[640,128]{1,0:T(8,128)S(1)}, f32[640,128]{1,0:T(8,128)S(1)}, u32[]{:S(2)}, u32[]{:S(2)}) collective-permute-start(f32[640,128]{1,0:T(8,128)S(1)} %get-tuple-element.20), channel_id=1, source_target_pairs={{1,0},{2,1},{3,2},{4,3},{5,4},{6,5},{7,6},{9,8},{10,9},{11,10},{12... | collective-permute-start | bytes 983048 | tf_op jit(solution)/shard_map/ppermute | solution.py:512
where the time goes:
time: 66 us; the launch traced here: 65.1 us
  starting transfers between devices  20.2 us (31%)
  blocking collectives  17.6 us (27%)
  Pallas kernels  17.4 us (26%)
  waiting for transfers between devices  9.73 us (15%)
    all_to_all x1, blocking collectives, regroup(): lax.all_to_all(chunks, 'ra', split_axis=0, concat_axis=0, tiled=True, axi...  17.6 us
    all_to_all x1, waiting for transfers between devices, regroup(): lax.all_to_all(chunks, 'ra', split_axis=0, concat_axis=0, tiled=True, axi...  9.72 us
    ppermute x1, starting transfers between devices, local(): part = lax.ppermute(part, 'ra', across)  7.83 us
    pallas_call x1, Pallas kernels, local(): pl.pallas_call(functools.partial(inner_kernel, batch=batch), out_shape=(o...  6.82 us
    pallas_call x1, Pallas kernels, local(): pl.pallas_call(functools.partial(outer_kernel, batch=batch), out_shape=ou...  6.7 us
    ppermute x1, starting transfers between devices, local(): above = lax.ppermute(bottom, 'dec', down)  6.19 us
    all_to_all x1, starting transfers between devices, regroup(): lax.all_to_all(chunks, 'ra', split_axis=0, concat_axis=0, tiled=True, axi...  3.86 us
    pallas_call x4, Pallas kernels, call(): pl.pallas_call(kernel, out_shape=shapes, in_specs=[pl.BlockSpec(memory_sp...  3.85 us
  transfers between devices with their start and end apart: 5, of which 1 were waited for; matrix products, arithmetic and copies ran while one was open for 0% of the time, Pallas kernels for 13%

commit v1 on v0

--- a/solution.py
+++ b/solution.py
@@ -17,6 +17,7 @@
 ROWS = 64
 EDGE = 16
 OUT = 40
+STEP = 1024
 HALF = 40
 CHUNK = 2 * HALF
 edge_rows = tuple(range(0, EDGE)) + tuple(range(ROWS - EDGE, ROWS))
@@ -91,8 +92,8 @@
         gathers[s, :, 0] = used & (sigma == s) & (side == 0)
         gathers[s, :, LANES - 1] = used & (sigma == s) & (side == 1)
     return (
-        np.stack(boxcars).astype(ml_dtypes.bfloat16),
-        gathers.astype(ml_dtypes.bfloat16),
+        np.concatenate(boxcars, axis=1).astype(ml_dtypes.bfloat16),
+        np.concatenate(gathers, axis=1).astype(ml_dtypes.bfloat16),
     )
 
 
@@ -263,24 +264,25 @@
     source[at : at + 16, 2 * LANES :] = jnp.concatenate(beside, axis=0).astype(jnp.bfloat16)
 
 
-def smooth_ra(source, weights_ref, rows, pairs, channels_at, done, edges):
+def smooth_ra(source, weights_ref, rows, channels_at, done, edges):
     operand = jnp.concatenate([source[:, : 2 * LANES], source[:, LANES:]], axis=1)
     along = dot(operand, weights_ref[...])
-    half = done.shape[1]
-    for j, (pair, c) in enumerate(zip(pairs, channels_at)):
+    half = done.shape[2] // LANES // 2
+    for j, c in enumerate(channels_at):
         block = along[j * rows : (j + 1) * rows]
-        lanes = slice((j % 2) * LANES, (j % 2 + 1) * LANES)
+        lanes = pl.ds(pl.multiple_of(c * LANES, LANES), LANES)
         for s in range(3):
             high, low = split(block[:, s * LANES : (s + 1) * LANES])
-            done[s, pair, :rows, lanes] = high
-            done[s, pair, rows:, lanes] = low
+            done[s, :rows, lanes] = high
+            done[s, rows:, lanes] = low
         tile, slot = c // half, c % half
         edges[tile] = edges[tile] + pltpu.roll(block[:, 3 * LANES :], 2 * slot, 1)
 
 
-def smooth_dec(parts, s, pair):
-    both = sum(dot(weights[s], done[s, pair]) for weights, done in parts)
-    return both[:OUT] + both[OUT:]
+def smooth_dec(parts, s, out):
+    for at in range(0, out.shape[1], STEP):
+        both = sum(dot(weights[s], done[s, :, at : at + STEP]) for weights, done in parts)
+        out[:, at : at + STEP] = both[:OUT] + both[OUT:]
 
 
 def beside_squares(parts, box_ref, gather_ref):
@@ -293,15 +295,42 @@
     for s in range(3):
         both = sum(dot(weights[s], value) for weights, value in parts)
         smoothed = jnp.where(which == s, both[:OUT] + both[OUT:], smoothed)
-    smoothed = split(smoothed)
-    result = []
-    for b in range(2):
-        summed = dot(smoothed[0], box_ref[b]) + dot(smoothed[1], box_ref[b])
-        square = split(summed * summed)
-        result.append(
-            [dot(square[0], gather_ref[s]) + dot(square[1], gather_ref[s]) for s in range(3)]
-        )
-    return result
+    high, low = split(smoothed)
+    summed = dot(high, box_ref[...]) + dot(low, box_ref[...])
+    summed = jnp.concatenate([summed[:, : 2 * LANES], summed[:, 2 * LANES :]], axis=0)
+    high, low = split(summed * summed)
+    squares = dot(high, gather_ref[...]) + dot(low, gather_ref[...])
+    return [
+        [squares[b * OUT : (b + 1) * OUT, s * LANES : (s + 1) * LANES] for s in range(3)]
+        for b in range(2)
+    ]
+
+
+def boxcar_sums(smooth, rows, result):
+    channels = result.shape[1]
+    squares = [[], []]
+    for at in range(0, OUT, 8):
+        planes = {
+            c: smooth[at : at + 8, c * LANES : (c + 1) * LANES] for c in range(channels)
+        }
+
+        def total(places):
+            return functools.reduce(jnp.add, [planes[c] for c in places if c in planes])
+
+        triples = {c: total(range(c - 1, c + 2)) for c in range(-1, channels + 1)}
+        totals = [[None, None], [None, None]]
+        for c in range(channels):
+            terms = [triples[c - 2]] if c >= 1 else []
+            terms += [triples[c + 1]] + ([planes[c + 3]] if c + 3 < channels else [])
+            for b, value in enumerate((triples[c], functools.reduce(jnp.add, terms))):
+                if at < rows:
+                    result[b, c, at : at + 8, :] = value
+                square = value * value
+                before = totals[b][c % 2]
+                totals[b][c % 2] = square if before is None else before + square
+        for b in range(2):
+            squares[b].append(totals[b][0] + totals[b][1])
+    return [jnp.concatenate(square, axis=0) for square in squares]
 
 
 def snr_rows(parts, beside, outside, runs, targets, smooth, result, framed, sems):
@@ -315,36 +344,13 @@
     no_side = ((lane == 0) & (ra_at == 0)) | ((lane == LANES - 1) & (ra_at == ra_n - 1))
     rows = sum(run[1] for run in runs)
     copies = []
+    smooth_dec(parts, 0, smooth.at[0])
     for s in range(3):
-
-        def smooth_pair(pair, carry):
-            both = smooth_dec(parts, s, pair)
-            smooth[3 + 2 * pair] = both[:, :LANES]
-            smooth[4 + 2 * pair] = both[:, LANES:]
-            return carry
-
-        for k in range(3):
-            smooth[k] = jnp.zeros((OUT, LANES), jnp.float32)
-            smooth[3 + channels + k] = jnp.zeros((OUT, LANES), jnp.float32)
-        lax.fori_loop(0, channels // 2, smooth_pair, 0, unroll=4)
-
-        squares = [[], []]
-        for at in range(0, OUT, 8):
-            planes = [smooth[k, at : at + 8, :] for k in range(channels + 6)]
-            triples = [planes[k] + planes[k + 1] + planes[k + 2] for k in range(channels + 4)]
-            totals = [[None, None], [None, None]]
-            for c in range(channels):
-                wide = triples[c] + triples[c + 3] + planes[c + 6]
-                for b, value in enumerate((triples[c + 2], wide)):
-                    if at < rows:
-                        result[2 * s + b, c, at : at + 8, :] = value
-                    square = value * value
-                    total = totals[b][c % 2]
-                    totals[b][c % 2] = square if total is None else total + square
-            for b in range(2):
-                squares[b].append(totals[b][0] + totals[b][1])
+        if s < 2:
+            smooth_dec(parts, s + 1, smooth.at[(s + 1) % 2])
+        squares = boxcar_sums(smooth.at[s % 2], rows, result.at[pl.ds(2 * s, 2)])
         for b, width in enumerate(boxcar_widths):
-            square = jnp.where(gone, 0.0, jnp.concatenate(squares[b], axis=0))
+            square = jnp.where(gone, 0.0, squares[b])
             across = square + jnp.where(no_side | gone, 0.0, beside[b][s])
             across = across + jnp.where(lane == 0, 0.0, pltpu.roll(square, 1, 1))
             across = across + jnp.where(lane == LANES - 1, 0.0, pltpu.roll(square, LANES - 1, 1))
@@ -352,23 +358,19 @@
             at = 0
             for first, length, before, after in runs:
                 at = at + 8
-                framed[at : at + length] = across[first : first + length]
-                framed[at - 1 : at] = across[before : before + 1]
-                framed[at + length : at + length + 1] = across[after : after + 1]
+                framed[b, at : at + length] = across[first : first + length]
+                framed[b, at - 1 : at] = across[before : before + 1]
+                framed[b, at + length : at + length + 1] = across[after : after + 1]
                 boxed.append(
-                    framed[at - 1 : at - 1 + length]
-                    + framed[at : at + length]
-                    + framed[at + 1 : at + 1 + length]
+                    framed[b, at - 1 : at - 1 + length]
+                    + framed[b, at : at + length]
+                    + framed[b, at + 1 : at + 1 + length]
                 )
                 at = at + length + 8
             boxed = jnp.concatenate(boxed, axis=0) if len(boxed) > 1 else boxed[0]
             scale = 1.0 / jnp.sqrt(boxed / (9.0 * channels) + width * width * epsilon)
-
-            def normalize(c, carry):
+            for c in range(channels):
                 result[2 * s + b, c] = result[2 * s + b, c] * scale
-                return carry
-
-            lax.fori_loop(0, channels, normalize, 0, unroll=8)
             for k, (first, length, _, _) in enumerate(runs):
                 copy = pltpu.make_async_copy(
                     result.at[2 * s + b, :, pl.ds(first, length), :],
@@ -394,7 +396,7 @@
     for part, parts in enumerate(halves_of):
         half_z = near if part == 0 else 1 - near
         for step in range(channels // 2 // batch):
-            pairs, channels_at = [], []
+            channels_at = []
             for j in range(batch):
                 i = step * batch + j
                 for half, (ref, at) in enumerate(parts):
@@ -405,9 +407,8 @@
                             source.at[part], j * ROWS + 32 * half + 16 * k, main,
                             (packed, packed), (64 * k, 64 * k + 32),
                         )
-                pairs.append(4 * (i // 4) + 2 * half_z + (i % 4) // 2)
                 channels_at.append(8 * (i // 4) + 4 * half_z + i % 4)
-            smooth_ra(source.at[part], ra_ref, ROWS, pairs, channels_at, done_ref, edges_ref)
+            smooth_ra(source.at[part], ra_ref, ROWS, channels_at, done_ref, edges_ref)
     beside = beside_squares([(dec_ref, edges_ref)], box_ref, gather_ref)
 
     def targets(s, b):
@@ -426,12 +427,12 @@
     *, batch,
 ):
     del held_ref
-    channels = 2 * done_ref.shape[1]
+    channels = done_ref.shape[2] // LANES
     near = (lax.axis_index("ra") // 4) % 2
     dec_at, dec_n = lax.axis_index("dec"), lax.axis_size("dec")
     halo_edges[...] = jnp.zeros_like(halo_edges)
     for step in range(channels // batch):
-        pairs, channels_at = [], []
+        channels_at = []
         for j in range(batch):
             at = step * batch + j
             part, i = at // (channels // 2), at % (channels // 2)
@@ -444,11 +445,8 @@
                     (packed, packed), (lanes, lanes + 32),
                 )
             half_z = near if part == 0 else 1 - near
-            pairs.append(4 * (i // 4) + 2 * half_z + (i % 4) // 2)
             channels_at.append(8 * (i // 4) + 4 * half_z + i % 4)
-        smooth_ra(
-            source.at[step % 2], ra_ref, 2 * EDGE, pairs, channels_at, halo_done, halo_edges
-        )
+        smooth_ra(source.at[step % 2], ra_ref, 2 * EDGE, channels_at, halo_done, halo_edges)
     parts = [(dec_ref, done_ref), (dec_halo_ref, halo_done)]
     beside = beside_squares(
         [(dec_ref, edges_ref), (dec_halo_ref, halo_edges)], box_ref, gather_ref
@@ -516,16 +514,16 @@
     out = jax.ShapeDtypeStruct((3, 2, channels, ROWS, LANES), f32)
     batch = 8
     work = [
-        pltpu.VMEM((channels + 6, OUT, LANES), f32),
+        pltpu.VMEM((2, OUT, channels * LANES), f32),
         pltpu.VMEM((6, channels, 2 * EDGE, LANES), f32),
-        pltpu.VMEM((ROWS + 16, LANES), f32),
+        pltpu.VMEM((2, ROWS + 16, LANES), f32),
     ]
     params = pltpu.CompilerParams(vmem_limit_bytes=32 * 2**20)
     held, done, edges = pl.pallas_call(
         functools.partial(inner_kernel, batch=batch),
         out_shape=(
             out,
-            jax.ShapeDtypeStruct((3, channels // 2, 2 * ROWS, 2 * LANES), jnp.bfloat16),
+            jax.ShapeDtypeStruct((3, 2 * ROWS, channels * LANES), jnp.bfloat16),
             jax.ShapeDtypeStruct((2, ROWS, LANES), f32),
         ),
         in_specs=[vmem] * 7,
@@ -550,7 +548,7 @@
         out_specs=anywhere,
         scratch_shapes=[
             pltpu.VMEM((2, batch * 2 * EDGE, 3 * LANES), jnp.bfloat16),
-            pltpu.VMEM((3, channels // 2, 4 * EDGE, 2 * LANES), jnp.bfloat16),
+            pltpu.VMEM((3, 4 * EDGE, channels * LANES), jnp.bfloat16),
             pltpu.VMEM((2, 2 * EDGE, LANES), f32),
         ]
         + work

time: 66 us -> 62.6 us (0.948)
  Pallas kernels: 17.4 us -> 12.9 us
  waiting for transfers between devices: 9.73 us -> 11.4 us
    pallas_call x1, Pallas kernels: 6.7 us -> 4.32 us  [local(): pl.pallas_call(functools.partial(outer_kernel, batch=batch), out_shape=ou...]
    pallas_call x1, Pallas kernels: 6.82 us -> 4.74 us  [local(): pl.pallas_call(functools.partial(inner_kernel, batch=batch), out_shape=(o...]
    ppermute x1, waiting for transfers between devices: 0.01 us -> 1.66 us  [local(): below = lax.ppermute(top, 'dec', up)]
  transfers between devices with their start and end apart: 5 -> 5, of which waited for: 1 -> 2; matrix products, arithmetic and copies ran while one was open for 0% -> 0% of each run, Pallas kernels for 13% -> 10%
where the time goes in v1:
time: 62.6 us; the launch traced here: 62.3 us
  starting transfers between devices  20.2 us (32%)
  blocking collectives  17.6 us (28%)
  Pallas kernels  12.9 us (21%)
  waiting for transfers between devices  11.4 us (18%)
    all_to_all x1, blocking collectives, regroup(): lax.all_to_all(chunks, 'ra', split_axis=0, concat_axis=0, tiled=True, axi...  17.6 us
    all_to_all x1, waiting for transfers between devices, regroup(): lax.all_to_all(chunks, 'ra', split_axis=0, concat_axis=0, tiled=True, axi...  9.72 us
    ppermute x1, starting transfers between devices, local(): part = lax.ppermute(part, 'ra', across)  7.83 us
    ppermute x1, starting transfers between devices, local(): above = lax.ppermute(bottom, 'dec', down)  6.19 us
    pallas_call x1, Pallas kernels, local(): pl.pallas_call(functools.partial(inner_kernel, batch=batch), out_shape=(o...  4.74 us
    pallas_call x1, Pallas kernels, local(): pl.pallas_call(functools.partial(outer_kernel, batch=batch), out_shape=ou...  4.32 us
    all_to_all x1, starting transfers between devices, regroup(): lax.all_to_all(chunks, 'ra', split_axis=0, concat_axis=0, tiled=True, axi...  3.86 us
    pallas_call x4, Pallas kernels, call(): pl.pallas_call(kernel, out_shape=shapes, in_specs=[pl.BlockSpec(memory_sp...  3.85 us
  transfers between devices with their start and end apart: 5, of which 2 were waited for; matrix products, arithmetic and copies ran while one was open for 0% of the time, Pallas kernels for 10%

profile of v1, /device:TPU:1, one launch (start us, length us, event | category | flops | bytes accessed | tf_op | source)
XLA Modules:
  0.0 62.3 jit_solution(104530139186251843)
XLA Ops:
  0.0 0.0 copy-start
  0.0 0.0 copy-start.2
  0.0 0.0 copy-start.1
  0.0 0.0 copy-start.5
  0.0 1.3 %columns.1 = (f32[17,32,128]{2,1,0:T(8,128)S(1)}, f32[17,32,128]{2,1,0:T(8,128)S(1)}) custom-call(f32[1,64,4096]{2,1,0:T(8,128)} %cube_ref.2), custom_call_target="tpu_custom_call" | custom-call | tf_op jit(solution)/shard_map/columns/pallas_call | solution.py:468
  1.3 7.8 %collective-permute-start = (f32[17,32,128]{2,1,0:T(8,128)S(1)}, f32[17,32,128]{2,1,0:T(8,128)S(1)}, u32[]{:S(2)}, u32[]{:S(2)}) collective-permute-start(f32[17,32,128]{2,1,0:T(8,128)S(1)} %get-tuple-element.16), channel_id=1, source_target_pairs={{0,32},{8,40},{16,48},{24,56},{32,0},{40,8},{48,16},{56,24},{64,96... | collective-permute-start | bytes 835592 | tf_op jit(solution)/shard_map/ppermute | solution.py:491
  9.2 18.9 %conditional.1 = (f32[16,80,128]{2,1,0:T(8,128)S(1)}) conditional(s32[]{:T(128)} %convert_element_type.3, () %tuple.11, f32[1,64,4096]{2,1,0:T(8,128)} %cube_ref.2), branch_computations={%region_0.0_spmd, %region_1.0_spmd} | conditional | bytes 1310728 | solution.py:500
  9.2 1.3 %middle.1 = f32[16,80,128]{2,1,0:T(8,128)S(1)} custom-call(f32[1,64,4096]{2,1,0:T(8,128)} %cube_ref.1), custom_call_target="tpu_custom_call" | custom-call | tf_op jit(solution)/shard_map/cond/branch_1_fun/middle/pallas_call | solution.py:468
  10.5 17.6 %all_to_all.9 = f32[16,80,128]{2,1,0:T(8,128)S(1)} all-to-all(f32[16,80,128]{2,1,0:T(8,128)S(1)} %middle.1), channel_id=1, replica_groups={{0,8,16,24,64,72,80,88,128,136,144,152,192,200,208,216},{32,40,48,56,96..., dimensions={0} | all-to-all | bytes 1310720 | tf_op jit(solution)/shard_map/cond/branch_1_fun/all_to_all | solution.py:482
  28.1 0.0 copy-start.3
  28.1 0.0 copy-start.4
  28.1 0.0 collective-permute-done.far_ref
  28.1 1.1 %edge_rows.1 = f32[16,80,128]{2,1,0:T(8,128)} custom-call(f32[16,80,128]{2,1,0:T(8,128)S(1)} %get-tuple-element.23.after_ref.middle_ref, f32[17,32,128]{2,1,0:T(8,128)S(1)} %collective-permute-done.far_ref, f32[17,32,128]{2,1,0:T(8,128)S(1)} %get-tuple-element.17.near_ref), custom_call_target="tpu_custom_call" | custom-call | tf_op jit(solution)/shard_map/edge_rows/pallas_call | solution.py:468
  29.2 3.9 %all-to-all-start.1 = ((f32[16,80,128]{2,1,0:T(8,128)}), f32[16,80,128]{2,1,0:T(8,128)S(1)}, u32[]{:S(2)}, u32[]{:S(2)}) async-start(f32[16,80,128]{2,1,0:T(8,128)} %edge_rows.1), calls=%async_computation.1 | async-start | bytes 1310720 | tf_op jit(solution)/shard_map/all_to_all | solution.py:482
  33.1 0.4 collective-permute-start.1
  33.5 9.7 %all-to-all-done.1.edge_ref = f32[16,80,128]{2,1,0:T(8,128)S(1)} async-done(((f32[16,80,128]{2,1,0:T(8,128)}), f32[16,80,128]{2,1,0:T(8,128)S(1)}, u32[]{:S(2)}, u32[]{:S(2)}) %all-to-all-start.1) | async-done | bytes 655392 | tf_op jit(solution)/shard_map/all_to_all | solution.py:482
  43.3 0.1 edges.1
  43.4 6.2 %collective-permute-start.2 = (f32[640,128]{1,0:T(8,128)S(1)}, f32[640,128]{1,0:T(8,128)S(1)}, u32[]{:S(2)}, u32[]{:S(2)}) collective-permute-start(f32[640,128]{1,0:T(8,128)S(1)} %get-tuple-element.19), channel_id=1, source_target_pairs={{0,1},{1,2},{2,3},{3,4},{4,5},{5,6},{6,7},{8,9},{9,10},{10,11},{11... | collective-permute-start | bytes 983048 | tf_op jit(solution)/shard_map/ppermute | solution.py:509
  49.6 1.9 %collective-permute-start.3 = (f32[640,128]{1,0:T(8,128)S(1)}, f32[640,128]{1,0:T(8,128)S(1)}, u32[]{:S(2)}, u32[]{:S(2)}) collective-permute-start(f32[640,128]{1,0:T(8,128)S(1)} %get-tuple-element.20), channel_id=1, source_target_pairs={{1,0},{2,1},{3,2},{4,3},{5,4},{6,5},{7,6},{9,8},{10,9},{11,10},{12... | collective-permute-start | bytes 983048 | tf_op jit(solution)/shard_map/ppermute | solution.py:510
  51.5 0.0 collective-permute-done.1.far_middle_ref
  51.5 0.0 copy-done
  51.5 0.0 copy-done.2
  51.5 0.0 copy-done.1
  51.5 0.0 copy-done.5
  51.6 4.7 %inner.1 = (f32[3,2,32,64,128]{4,3,2,1,0:T(8,128)}, bf16[3,128,4096]{2,1,0:T(8,128)(2,1)S(1)}, f32[2,64,128]{2,1,0:T(8,128)S(1)}) custom-call(f32[16,80,128]{2,1,0:T(8,128)S(1)} %all-to-all-done.1.edge_ref, f32[16,80,128]{2,1,0:T(8,128)S(1)} %get-tuple-element.23.after_ref.middle_ref, f32[16,40,128]{2,1,0:T(8,128)S(1)} %collective-permute-done.1.far_middle_ref, ...), custom_call_target="tpu_custom_call" | custom-call | flops 2000000000 | bytes 8388608 | tf_op jit(solution)/shard_map/inner/pallas_call | solution.py:522
  56.3 0.0 collective-permute-done.2.above_ref
  56.3 1.7 %collective-permute-done.3.below_ref = f32[640,128]{1,0:T(8,128)S(1)} collective-permute-done((f32[640,128]{1,0:T(8,128)S(1)}, f32[640,128]{1,0:T(8,128)S(1)}, u32[]{:S(2)}, u32[]{:S(2)}) %collective-permute-start.3) | collective-permute-done | bytes 327712 | tf_op jit(solution)/shard_map/ppermute | solution.py:510
  58.0 0.0 copy-done.3
  58.0 0.0 copy-done.4
  58.0 4.3 %outer.1 = f32[3,2,32,64,128]{4,3,2,1,0:T(8,128)} custom-call(f32[3,2,32,64,128]{4,3,2,1,0:T(8,128)} %get-tuple-element.18.held_ref, f32[640,128]{1,0:T(8,128)S(1)} %collective-permute-done.2.above_ref, f32[640,128]{1,0:T(8,128)S(1)} %collective-permute-done.3.below_ref, ...), custom_call_target="tpu_custom_call", output_to_operand_aliasing={{}: (0, {})} | custom-call | flops 1000000000 | bytes 8388608 | tf_op jit(solution)/shard_map/outer/pallas_call | solution.py:544
  (1 shorter events, 0.0 us)
Async XLA Ops:
  0.0 51.5 %copy-start = (bf16[512,512]{1,0:T(8,128)(2,1)S(1)}, bf16[512,512]{1,0:T(8,128)(2,1)}, u32[]{:S(2)}) copy-start(bf16[512,512]{1,0:T(8,128)(2,1)} %constant.24.clone.ra_ref) | copy-start | bytes 1572868
  0.0 51.5 %copy-start.2 = (bf16[256,384]{1,0:T(8,128)(2,1)S(1)}, bf16[256,384]{1,0:T(8,128)(2,1)}, u32[]{:S(2)}) copy-start(bf16[256,384]{1,0:T(8,128)(2,1)} %constant.23.clone.gather_ref) | copy-start | bytes 589828
  0.0 51.5 %copy-start.1 = (bf16[256,512]{1,0:T(8,128)(2,1)S(1)}, bf16[256,512]{1,0:T(8,128)(2,1)}, u32[]{:S(2)}) copy-start(bf16[256,512]{1,0:T(8,128)(2,1)} %constant.22.clone.box_ref) | copy-start | bytes 786436
  0.0 51.5 %copy-start.5 = (bf16[3,80,128]{2,1,0:T(8,128)(2,1)S(1)}, bf16[3,80,128]{2,1,0:T(8,128)(2,1)}, u32[]{:S(2)}) copy-start(bf16[3,80,128]{2,1,0:T(8,128)(2,1)} %constant.25.clone.dec_ref) | copy-start | bytes 184324
  1.3 26.8 %collective-permute-start = (f32[17,32,128]{2,1,0:T(8,128)S(1)}, f32[17,32,128]{2,1,0:T(8,128)S(1)}, u32[]{:S(2)}, u32[]{:S(2)}) collective-permute-start(f32[17,32,128]{2,1,0:T(8,128)S(1)} %get-tuple-element.16), channel_id=1, source_target_pairs={{0,32},{8,40},{16,48},{24,56},{32,0},{40,8},{48,16},{56,24},{64,96... | collective-permute-start | bytes 835592 | tf_op jit(solution)/shard_map/ppermute | solution.py:491
  28.1 29.9 %copy-start.3 = (bf16[3,80,64]{2,1,0:T(8,128)(2,1)S(1)}, bf16[3,80,64]{2,1,0:T(8,128)(2,1)}, u32[]{:S(2)}) copy-start(bf16[3,80,64]{2,1,0:T(8,128)(2,1)} %constant.27.clone.dec_halo_ref) | copy-start | bytes 92164
  28.1 29.9 %copy-start.4 = (bf16[3,80,128]{2,1,0:T(8,128)(2,1)S(1)}, bf16[3,80,128]{2,1,0:T(8,128)(2,1)}, u32[]{:S(2)}) copy-start(bf16[3,80,128]{2,1,0:T(8,128)(2,1)} %constant.26.clone.dec_ref) | copy-start | bytes 184324
  29.2 14.1 %all-to-all-start.1 = ((f32[16,80,128]{2,1,0:T(8,128)}), f32[16,80,128]{2,1,0:T(8,128)S(1)}, u32[]{:S(2)}, u32[]{:S(2)}) async-start(f32[16,80,128]{2,1,0:T(8,128)} %edge_rows.1), calls=%async_computation.1 | async-start | bytes 1310720 | tf_op jit(solution)/shard_map/all_to_all | solution.py:482
  33.1 18.4 %collective-permute-start.1 = (f32[16,40,128]{2,1,0:T(8,128)S(1)}, f32[16,40,128]{2,1,0:T(8,128)S(1)}, u32[]{:S(2)}, u32[]{:S(2)}) collective-permute-start(f32[16,40,128]{2,1,0:T(8,128)S(1)} %slice.4), channel_id=1, source_target_pairs={{0,32},{8,40},{16,48},{24,56},{32,0},{40,8},{48,16},{56,24},{64,96... | collective-permute-start | bytes 983048 | tf_op jit(solution)/shard_map/ppermute | solution.py:501
  43.4 12.9 %collective-permute-start.2 = (f32[640,128]{1,0:T(8,128)S(1)}, f32[640,128]{1,0:T(8,128)S(1)}, u32[]{:S(2)}, u32[]{:S(2)}) collective-permute-start(f32[640,128]{1,0:T(8,128)S(1)} %get-tuple-element.19), channel_id=1, source_target_pairs={{0,1},{1,2},{2,3},{3,4},{4,5},{5,6},{6,7},{8,9},{9,10},{10,11},{11... | collective-permute-start | bytes 983048 | tf_op jit(solution)/shard_map/ppermute | solution.py:509
  49.6 8.4 %collective-permute-start.3 = (f32[640,128]{1,0:T(8,128)S(1)}, f32[640,128]{1,0:T(8,128)S(1)}, u32[]{:S(2)}, u32[]{:S(2)}) collective-permute-start(f32[640,128]{1,0:T(8,128)S(1)} %get-tuple-element.20), channel_id=1, source_target_pairs={{1,0},{2,1},{3,2},{4,3},{5,4},{6,5},{7,6},{9,8},{10,9},{11,10},{12... | collective-permute-start | bytes 983048 | tf_op jit(solution)/shard_map/ppermute | solution.py:510

commit v2 on v1

--- a/solution.py
+++ b/solution.py
@@ -23,7 +23,7 @@
 edge_rows = tuple(range(0, EDGE)) + tuple(range(ROWS - EDGE, ROWS))
 middle_rows = tuple(range(EDGE, ROWS - EDGE))
 tile_rows = edge_rows + middle_rows
-halo_rows = tuple(range(-EDGE, 0)) + tuple(range(ROWS, ROWS + EDGE))
+above_rows, below_rows = tuple(range(-EDGE, 0)), tuple(range(ROWS, ROWS + EDGE))
 inner_out = middle_rows + (EDGE - 1, ROWS - EDGE)
 outer_out = edge_rows + (-1, EDGE, ROWS - EDGE - 1, ROWS)
 inner_runs = ((0, 32, 32, 33),)
@@ -232,21 +232,24 @@
                 pack_rows((here, right, left), out_ref, tile, start)
 
 
-def edge_kernel(edge_ref, top_ref, bottom_ref):
+def edge_kernel(edge_ref, chip_ref, next_ref):
+    odd = lax.axis_index("dec") % 2
     count = edge_ref.shape[0]
     channels = 2 * count
     lane = lane_index((8, LANES))
-    for part, start in enumerate((HALF, 0)):
-        for i in range(count):
-            at = (part * count + i) * EDGE
-            top_ref[at : at + EDGE, :] = edge_ref[i, start : start + EDGE, :]
-            bottom_ref[at : at + EDGE, :] = edge_ref[i, start + EDGE : start + 2 * EDGE, :]
-        for pair in range(count // 2):
-            at = channels * EDGE + 8 * (part * count // 2 + pair)
-            first = edge_ref[2 * pair, start + 32 : start + HALF, :]
-            second = edge_ref[2 * pair + 1, start + 32 : start + HALF, :]
-            top_ref[at : at + 8, :] = jnp.where(lane < 64, first, pltpu.roll(second, 64, 1))
-            bottom_ref[at : at + 8, :] = jnp.where(lane < 64, pltpu.roll(first, 64, 1), second)
+    for ref, lower in ((chip_ref, 1 - odd), (next_ref, odd)):
+        rows = pl.multiple_of(EDGE * lower, EDGE)
+        for part, start in enumerate((HALF, 0)):
+            for i in range(count):
+                at = (part * count + i) * EDGE
+                ref[at : at + EDGE, :] = edge_ref[i, pl.ds(start + rows, EDGE), :]
+            for pair in range(count // 2):
+                at = channels * EDGE + 8 * (part * count // 2 + pair)
+                first = edge_ref[2 * pair, start + 32 : start + HALF, :]
+                second = edge_ref[2 * pair + 1, start + 32 : start + HALF, :]
+                upper_halves = jnp.where(lane < 64, first, pltpu.roll(second, 64, 1))
+                lower_halves = jnp.where(lane < 64, pltpu.roll(first, 64, 1), second)
+                ref[at : at + 8, :] = jnp.where(lower == 1, lower_halves, upper_halves)
 
 
 def put_rows(source, at, main, packed, places):
@@ -420,7 +423,7 @@
 
 
 def outer_kernel(
-    held_ref, above_ref, below_ref, done_ref, edges_ref,
+    held_ref, chip_ref, next_ref, done_ref, edges_ref,
     ra_ref, dec_ref, dec_halo_ref, box_ref, gather_ref,
     out_ref,
     source, halo_done, halo_edges, smooth, result, framed, sems,
@@ -436,7 +439,7 @@
         for j in range(batch):
             at = step * batch + j
             part, i = at // (channels // 2), at % (channels // 2)
-            for k, ref in enumerate((above_ref, below_ref)):
+            for k, ref in enumerate((chip_ref, next_ref)):
                 row = channels * EDGE + 8 * (at // 2)
                 packed = ref[row : row + 8, :]
                 lanes = 64 * (at % 2)
@@ -447,6 +450,7 @@
             half_z = near if part == 0 else 1 - near
             channels_at.append(8 * (i // 4) + 4 * half_z + i % 4)
         smooth_ra(source.at[step % 2], ra_ref, 2 * EDGE, channels_at, halo_done, halo_edges)
+    dec_halo_ref = dec_halo_ref.at[dec_at % 2]
     parts = [(dec_ref, done_ref), (dec_halo_ref, halo_done)]
     beside = beside_squares(
         [(dec_ref, edges_ref), (dec_halo_ref, halo_edges)], box_ref, gather_ref
@@ -499,15 +503,24 @@
 
     middle = lax.cond(lax.axis_index("ra") >= 0, regroup_middle, nothing, cube)
     far_middle = lax.ppermute(middle[:, :HALF], "ra", across)
-    edge = call(edge_rows_kernel, chunk, (part, near_part), "edge_rows", (middle,))
-    edge_chunk = regroup(edge)
+
+    def regroup_edges(part, near_part, middle):
+        chunks = call(edge_rows_kernel, chunk, (part, near_part), "edge_rows", (middle,))
+        chunks = regroup(chunks)
+        return (chunks, *call(edge_kernel, (edge, edge), (chunks,), "edges"))
+
+    def no_edges(part, near_part, middle):
+        return jnp.zeros(chunk.shape, f32), jnp.zeros(edge.shape, f32), jnp.zeros(edge.shape, f32)
+
     edge = jax.ShapeDtypeStruct((channels * (EDGE + 4), LANES), f32)
-    top, bottom = call(edge_kernel, (edge, edge), (edge_chunk,), "edges")
+    edge_chunk, for_chip, for_next = lax.cond(
+        lax.axis_index("ra") >= 0, regroup_edges, no_edges, part, near_part, middle
+    )
     count = lax.axis_size("dec")
-    down = [(i, i + 1) for i in range(count - 1)]
-    up = [(i + 1, i) for i in range(count - 1)]
-    above = lax.ppermute(bottom, "dec", down)
-    below = lax.ppermute(top, "dec", up)
+    on_chip = [(i, i ^ 1) for i in range(count)]
+    beyond = [(i, i + 1) for i in range(1, count - 1, 2)] + [(i + 1, i) for i in range(1, count - 1, 2)]
+    from_chip = lax.ppermute(for_chip, "dec", on_chip)
+    from_next = lax.ppermute(for_next, "dec", beyond)
     box, gather = (jnp.asarray(value) for value in edge_weights(channels))
     along = jnp.asarray(ra_weights())
     anywhere = pl.BlockSpec(memory_space=pl.ANY)
@@ -541,6 +554,9 @@
         jnp.asarray(dec_weights(inner_out, tile_rows)), box, gather,
     )
     batch = 16
+    halo_weights = np.stack(
+        [dec_weights(outer_out, rows) for rows in (below_rows + above_rows, above_rows + below_rows)]
+    )
     return pl.pallas_call(
         functools.partial(outer_kernel, batch=batch),
         out_shape=out,
@@ -560,9 +576,9 @@
         ),
         name="outer",
     )(
-        held, above, below, done, edges, along,
+        held, from_chip, from_next, done, edges, along,
         jnp.asarray(dec_weights(outer_out, tile_rows)),
-        jnp.asarray(dec_weights(outer_out, halo_rows)), box, gather,
+        jnp.asarray(halo_weights), box, gather,
     )
 
 

time: 62.6 us -> 60.6 us (0.968)
  blocking collectives: 17.6 us -> 31.1 us
  waiting for transfers between devices: 11.4 us -> 0.01 us
  starting transfers between devices: 20.2 us -> 14.8 us
  Pallas kernels: 12.9 us -> 14.1 us
    all_to_all x1 -> x2, blocking collectives: 17.6 us -> 31.1 us  [regroup(): lax.all_to_all(chunks, 'ra', split_axis=0, concat_axis=0, tiled=True, axi...]
    all_to_all x1 -> x0, waiting for transfers between devices: 9.72 us -> none  [regroup(): lax.all_to_all(chunks, 'ra', split_axis=0, concat_axis=0, tiled=True, axi...]
    all_to_all x1 -> x0, starting transfers between devices: 3.86 us -> none  [regroup(): lax.all_to_all(chunks, 'ra', split_axis=0, concat_axis=0, tiled=True, axi...]
    ppermute x2, starting transfers between devices: 8.11 us -> 6.28 us  [the longest x1 3.73 us: local(): from_chip = lax.ppermute(for_chip, 'dec', on_chip)]
    ppermute x2, waiting for transfers between devices: 1.66 us -> 0.01 us  [the longest x1 0.01 us: local(): from_chip = lax.ppermute(for_chip, 'dec', on_chip)]
    pallas_call x1, Pallas kernels: 4.74 us -> 5.77 us  [local(): pl.pallas_call(functools.partial(inner_kernel, batch=batch), out_shape=(o...]
  transfers between devices with their start and end apart: 5 -> 4, of which waited for: 2 -> 0; matrix products, arithmetic and copies ran while one was open for 0% -> 0% of each run, Pallas kernels for 10% -> 14%
where the time goes in v2:
time: 60.6 us; the launch traced here: 60.3 us
  blocking collectives  31.1 us (51%)
  starting transfers between devices  14.8 us (24%)
  Pallas kernels  14.1 us (23%)
    all_to_all x2, blocking collectives, regroup(): lax.all_to_all(chunks, 'ra', split_axis=0, concat_axis=0, tiled=True, axi...  31.1 us
    ppermute x1, starting transfers between devices, local(): part = lax.ppermute(part, 'ra', across)  7.83 us
    pallas_call x1, Pallas kernels, local(): pl.pallas_call(functools.partial(inner_kernel, batch=batch), out_shape=(o...  5.77 us
    pallas_call x1, Pallas kernels, local(): pl.pallas_call(functools.partial(outer_kernel, batch=batch), out_shape=ou...  4.24 us
    pallas_call x4, Pallas kernels, call(): pl.pallas_call(kernel, out_shape=shapes, in_specs=[pl.BlockSpec(memory_sp...  4.13 us
    ppermute x1, starting transfers between devices, local(): from_chip = lax.ppermute(for_chip, 'dec', on_chip)  3.73 us
    ppermute x1, starting transfers between devices, local(): from_next = lax.ppermute(for_next, 'dec', beyond)  2.55 us
  transfers between devices with their start and end apart: 4, of which 0 were waited for; matrix products, arithmetic and copies ran while one was open for 0% of the time, Pallas kernels for 14%

profile of v2, /device:TPU:1, one launch (start us, length us, event | category | flops | bytes accessed | tf_op | source)
XLA Modules:
  0.0 60.3 jit_solution(6292906532301591008)
XLA Ops:
  0.0 0.0 copy-start
  0.0 0.0 copy-start.2
  0.0 0.0 copy-start.1
  0.0 0.0 copy-start.5
  0.0 1.3 %columns.1 = (f32[17,32,128]{2,1,0:T(8,128)S(1)}, f32[17,32,128]{2,1,0:T(8,128)S(1)}) custom-call(f32[1,64,4096]{2,1,0:T(8,128)} %cube_ref.2), custom_call_target="tpu_custom_call" | custom-call | tf_op jit(solution)/shard_map/columns/pallas_call | solution.py:472
  1.3 7.8 %collective-permute-start = (f32[17,32,128]{2,1,0:T(8,128)S(1)}, f32[17,32,128]{2,1,0:T(8,128)S(1)}, u32[]{:S(2)}, u32[]{:S(2)}) collective-permute-start(f32[17,32,128]{2,1,0:T(8,128)S(1)} %get-tuple-element.28), channel_id=1, source_target_pairs={{0,32},{8,40},{16,48},{24,56},{32,0},{40,8},{48,16},{56,24},{64,96... | collective-permute-start | bytes 835592 | tf_op jit(solution)/shard_map/ppermute | solution.py:495
  9.2 18.9 %conditional.2 = (f32[16,80,128]{2,1,0:T(8,128)S(1)}) conditional(s32[]{:T(128)} %convert_element_type.4, () %tuple.20, f32[1,64,4096]{2,1,0:T(8,128)} %cube_ref.2), branch_computations={%region_0.0_spmd, %region_1.0_spmd} | conditional | bytes 1310728 | solution.py:504
  9.2 1.3 %middle.1 = f32[16,80,128]{2,1,0:T(8,128)S(1)} custom-call(f32[1,64,4096]{2,1,0:T(8,128)} %cube_ref.1), custom_call_target="tpu_custom_call" | custom-call | tf_op jit(solution)/shard_map/cond/branch_1_fun/middle/pallas_call | solution.py:472
  10.5 17.6 %all_to_all.8 = f32[16,80,128]{2,1,0:T(8,128)S(1)} all-to-all(f32[16,80,128]{2,1,0:T(8,128)S(1)} %middle.1), channel_id=1, replica_groups={{0,8,16,24,64,72,80,88,128,136,144,152,192,200,208,216},{32,40,48,56,96..., dimensions={0} | all-to-all | bytes 1310720 | tf_op jit(solution)/shard_map/cond/branch_1_fun/all_to_all | solution.py:486
  28.1 0.0 copy-start.3
  28.1 0.0 copy-start.4
  28.1 0.7 %collective-permute-start.1 = (f32[16,40,128]{2,1,0:T(8,128)S(1)}, f32[16,40,128]{2,1,0:T(8,128)S(1)}, u32[]{:S(2)}, u32[]{:S(2)}) collective-permute-start(f32[16,40,128]{2,1,0:T(8,128)S(1)} %slice.4), channel_id=1, source_target_pairs={{0,32},{8,40},{16,48},{24,56},{32,0},{40,8},{48,16},{56,24},{64,96... | collective-permute-start | bytes 983048 | tf_op jit(solution)/shard_map/ppermute | solution.py:505
  28.8 0.0 collective-permute-done
  28.8 15.0 %conditional.3 = (f32[16,80,128]{2,1,0:T(8,128)}, f32[640,128]{1,0:T(8,128)S(1)}, f32[640,128]{1,0:T(8,128)S(1)}) conditional(s32[]{:T(128)} %convert_element_type.4, () %tuple.19, (f32[16,80,128]{2,1,0:T(8,128)S(1)}, f32[17,32,128]{2,1,0:T(8,128)S(1)}, f32[17,32,128]{2,1,0:T(8,128)S(1)}) %tuple.21), branch_computations={%region_2.0_spmd, %region_3.0_spmd} | conditional | bytes 1310756 | solution.py:516
  28.9 0.3 edge_rows.1
  29.1 13.5 %all_to_all.9.edge_ref = f32[16,80,128]{2,1,0:T(8,128)} all-to-all(f32[16,80,128]{2,1,0:T(8,128)S(1)} %edge_rows.1), channel_id=1, replica_groups={{0,8,16,24,64,72,80,88,128,136,144,152,192,200,208,216},{32,40,48,56,96..., dimensions={0} | all-to-all | bytes 1310720 | tf_op jit(solution)/shard_map/cond/branch_1_fun/all_to_all | solution.py:486
  42.7 1.2 %edges.1 = (f32[640,128]{1,0:T(8,128)S(1)}, f32[640,128]{1,0:T(8,128)S(1)}) custom-call(f32[16,80,128]{2,1,0:T(8,128)} %all_to_all.9.edge_ref), custom_call_target="tpu_custom_call" | custom-call | tf_op jit(solution)/shard_map/cond/branch_1_fun/edges/pallas_call | solution.py:472
  43.9 3.7 %collective-permute-start.2 = (f32[640,128]{1,0:T(8,128)S(1)}, f32[640,128]{1,0:T(8,128)S(1)}, u32[]{:S(2)}, u32[]{:S(2)}) collective-permute-start(f32[640,128]{1,0:T(8,128)S(1)} %get-tuple-element.32), channel_id=1, source_target_pairs={{0,1},{1,0},{2,3},{3,2},{4,5},{5,4},{6,7},{7,6},{8,9},{9,8},{10,11... | collective-permute-start | bytes 983048 | tf_op jit(solution)/shard_map/ppermute | solution.py:522
  47.6 2.5 %collective-permute-start.3 = (f32[640,128]{1,0:T(8,128)S(1)}, f32[640,128]{1,0:T(8,128)S(1)}, u32[]{:S(2)}, u32[]{:S(2)}) collective-permute-start(f32[640,128]{1,0:T(8,128)S(1)} %get-tuple-element.33), channel_id=1, source_target_pairs={{1,2},{3,4},{5,6},{2,1},{4,3},{6,5},{9,10},{11,12},{13,14},{10,9},... | collective-permute-start | bytes 983048 | tf_op jit(solution)/shard_map/ppermute | solution.py:523
  50.2 0.0 collective-permute-done.1.far_middle_ref
  50.2 0.0 copy-done
  50.2 0.0 copy-done.2
  50.2 0.0 copy-done.1
  50.2 0.0 copy-done.5
  50.2 5.8 %inner.1 = (f32[3,2,32,64,128]{4,3,2,1,0:T(8,128)}, bf16[3,128,4096]{2,1,0:T(8,128)(2,1)S(1)}, f32[2,64,128]{2,1,0:T(8,128)S(1)}) custom-call(f32[16,80,128]{2,1,0:T(8,128)} %get-tuple-element.30.edge_ref, f32[16,80,128]{2,1,0:T(8,128)S(1)} %get-tuple-element.42.middle_ref, f32[16,40,128]{2,1,0:T(8,128)S(1)} %collective-permute-done.1.far_middle_ref, ...), custom_call_target="tpu_custom_call" | custom-call | flops 2000000000 | bytes 8388608 | tf_op jit(solution)/shard_map/inner/pallas_call | solution.py:535
  56.0 0.0 collective-permute-done.2.chip_ref
  56.0 0.0 collective-permute-done.3.next_ref
  56.0 0.0 copy-done.3
  56.0 0.0 copy-done.4
  56.0 4.2 %outer.1 = f32[3,2,32,64,128]{4,3,2,1,0:T(8,128)} custom-call(f32[3,2,32,64,128]{4,3,2,1,0:T(8,128)} %get-tuple-element.31.held_ref, f32[640,128]{1,0:T(8,128)S(1)} %collective-permute-done.2.chip_ref, f32[640,128]{1,0:T(8,128)S(1)} %collective-permute-done.3.next_ref, ...), custom_call_target="tpu_custom_call", output_to_operand_aliasing={{}: (0, {})} | custom-call | flops 1000000000 | bytes 8388608 | tf_op jit(solution)/shard_map/outer/pallas_call | solution.py:560
  (1 shorter events, 0.0 us)
Async XLA Ops:
  0.0 50.2 %copy-start = (bf16[512,512]{1,0:T(8,128)(2,1)S(1)}, bf16[512,512]{1,0:T(8,128)(2,1)}, u32[]{:S(2)}) copy-start(bf16[512,512]{1,0:T(8,128)(2,1)} %constant.27.clone.ra_ref) | copy-start | bytes 1572868
  0.0 50.2 %copy-start.2 = (bf16[256,384]{1,0:T(8,128)(2,1)S(1)}, bf16[256,384]{1,0:T(8,128)(2,1)}, u32[]{:S(2)}) copy-start(bf16[256,384]{1,0:T(8,128)(2,1)} %constant.26.clone.gather_ref) | copy-start | bytes 589828
  0.0 50.2 %copy-start.1 = (bf16[256,512]{1,0:T(8,128)(2,1)S(1)}, bf16[256,512]{1,0:T(8,128)(2,1)}, u32[]{:S(2)}) copy-start(bf16[256,512]{1,0:T(8,128)(2,1)} %constant.25.clone.box_ref) | copy-start | bytes 786436
  0.0 50.2 %copy-start.5 = (bf16[3,80,128]{2,1,0:T(8,128)(2,1)S(1)}, bf16[3,80,128]{2,1,0:T(8,128)(2,1)}, u32[]{:S(2)}) copy-start(bf16[3,80,128]{2,1,0:T(8,128)(2,1)} %constant.28.clone.dec_ref) | copy-start | bytes 184324
  1.3 27.5 %collective-permute-start = (f32[17,32,128]{2,1,0:T(8,128)S(1)}, f32[17,32,128]{2,1,0:T(8,128)S(1)}, u32[]{:S(2)}, u32[]{:S(2)}) collective-permute-start(f32[17,32,128]{2,1,0:T(8,128)S(1)} %get-tuple-element.28), channel_id=1, source_target_pairs={{0,32},{8,40},{16,48},{24,56},{32,0},{40,8},{48,16},{56,24},{64,96... | collective-permute-start | bytes 835592 | tf_op jit(solution)/shard_map/ppermute | solution.py:495
  28.1 27.9 %copy-start.3 = (bf16[2,3,80,64]{3,2,1,0:T(8,128)(2,1)S(1)}, bf16[2,3,80,64]{3,2,1,0:T(8,128)(2,1)}, u32[]{:S(2)}) copy-start(bf16[2,3,80,64]{3,2,1,0:T(8,128)(2,1)} %constant.30.clone.dec_halo_ref) | copy-start | bytes 184324
  28.1 27.9 %copy-start.4 = (bf16[3,80,128]{2,1,0:T(8,128)(2,1)S(1)}, bf16[3,80,128]{2,1,0:T(8,128)(2,1)}, u32[]{:S(2)}) copy-start(bf16[3,80,128]{2,1,0:T(8,128)(2,1)} %constant.29.clone.dec_ref) | copy-start | bytes 184324
  28.1 22.0 %collective-permute-start.1 = (f32[16,40,128]{2,1,0:T(8,128)S(1)}, f32[16,40,128]{2,1,0:T(8,128)S(1)}, u32[]{:S(2)}, u32[]{:S(2)}) collective-permute-start(f32[16,40,128]{2,1,0:T(8,128)S(1)} %slice.4), channel_id=1, source_target_pairs={{0,32},{8,40},{16,48},{24,56},{32,0},{40,8},{48,16},{56,24},{64,96... | collective-permute-start | bytes 983048 | tf_op jit(solution)/shard_map/ppermute | solution.py:505
  43.9 12.1 %collective-permute-start.2 = (f32[640,128]{1,0:T(8,128)S(1)}, f32[640,128]{1,0:T(8,128)S(1)}, u32[]{:S(2)}, u32[]{:S(2)}) collective-permute-start(f32[640,128]{1,0:T(8,128)S(1)} %get-tuple-element.32), channel_id=1, source_target_pairs={{0,1},{1,0},{2,3},{3,2},{4,5},{5,4},{6,7},{7,6},{8,9},{9,8},{10,11... | collective-permute-start | bytes 983048 | tf_op jit(solution)/shard_map/ppermute | solution.py:522
  47.6 8.4 %collective-permute-start.3 = (f32[640,128]{1,0:T(8,128)S(1)}, f32[640,128]{1,0:T(8,128)S(1)}, u32[]{:S(2)}, u32[]{:S(2)}) collective-permute-start(f32[640,128]{1,0:T(8,128)S(1)} %get-tuple-element.33), channel_id=1, source_target_pairs={{1,2},{3,4},{5,6},{2,1},{4,3},{6,5},{9,10},{11,12},{13,14},{10,9},... | collective-permute-start | bytes 983048 | tf_op jit(solution)/shard_map/ppermute | solution.py:523

commit v3 on v2

--- a/solution.py
+++ b/solution.py
@@ -232,7 +232,10 @@
                 pack_rows((here, right, left), out_ref, tile, start)
 
 
-def edge_kernel(edge_ref, chip_ref, next_ref):
+def edge_kernel(outside_ref, chip_ref, next_ref, edge_ref, sem):
+    fetch = pltpu.make_async_copy(outside_ref, edge_ref, sem)
+    fetch.start()
+    fetch.wait()
     odd = lax.axis_index("dec") % 2
     count = edge_ref.shape[0]
     channels = 2 * count
@@ -270,16 +273,19 @@
 def smooth_ra(source, weights_ref, rows, channels_at, done, edges):
     operand = jnp.concatenate([source[:, : 2 * LANES], source[:, LANES:]], axis=1)
     along = dot(operand, weights_ref[...])
-    half = done.shape[2] // LANES // 2
-    for j, c in enumerate(channels_at):
+    beside = {}
+    for j, (i, half_z) in enumerate(channels_at):
+        c = 8 * (i // 4) + 4 * half_z + i % 4
         block = along[j * rows : (j + 1) * rows]
         lanes = pl.ds(pl.multiple_of(c * LANES, LANES), LANES)
         for s in range(3):
             high, low = split(block[:, s * LANES : (s + 1) * LANES])
             done[s, :rows, lanes] = high
             done[s, rows:, lanes] = low
-        tile, slot = c // half, c % half
-        edges[tile] = edges[tile] + pltpu.roll(block[:, 3 * LANES :], 2 * slot, 1)
+        value = turn(block[:, 3 * LANES :], 16 * (i // 4 % 2) + 2 * (i % 4))
+        beside[i // 8] = beside[i // 8] + value if i // 8 in beside else value
+    for tile, value in beside.items():
+        edges[tile] = edges[tile] + pltpu.roll(value, 8 * half_z, 1)
 
 
 def smooth_dec(parts, s, out):
@@ -336,7 +342,7 @@
     return [jnp.concatenate(square, axis=0) for square in squares]
 
 
-def snr_rows(parts, beside, outside, runs, targets, smooth, result, framed, sems):
+def snr_rows(parts, beside, outside, runs, smooth, result, framed, finished, last=None):
     channels = result.shape[1]
     ra_at, ra_n = lax.axis_index("ra"), lax.axis_size("ra")
     lane = lane_index((OUT, LANES))
@@ -346,12 +352,14 @@
         gone = gone | ((row == at) & condition)
     no_side = ((lane == 0) & (ra_at == 0)) | ((lane == LANES - 1) & (ra_at == ra_n - 1))
     rows = sum(run[1] for run in runs)
-    copies = []
     smooth_dec(parts, 0, smooth.at[0])
     for s in range(3):
-        if s < 2:
-            smooth_dec(parts, s + 1, smooth.at[(s + 1) % 2])
+        if s == 1:
+            smooth_dec(parts, 2, smooth.at[0])
         squares = boxcar_sums(smooth.at[s % 2], rows, result.at[pl.ds(2 * s, 2)])
+        if s == 0:
+            beside = beside()
+            smooth_dec(parts, 1, smooth.at[1])
         for b, width in enumerate(boxcar_widths):
             square = jnp.where(gone, 0.0, squares[b])
             across = square + jnp.where(no_side | gone, 0.0, beside[b][s])
@@ -372,23 +380,15 @@
                 at = at + length + 8
             boxed = jnp.concatenate(boxed, axis=0) if len(boxed) > 1 else boxed[0]
             scale = 1.0 / jnp.sqrt(boxed / (9.0 * channels) + width * width * epsilon)
+            kept = result.at[2 * s + b] if last is None or s < 2 else last.at[b]
             for c in range(channels):
-                result[2 * s + b, c] = result[2 * s + b, c] * scale
-            for k, (first, length, _, _) in enumerate(runs):
-                copy = pltpu.make_async_copy(
-                    result.at[2 * s + b, :, pl.ds(first, length), :],
-                    targets(s, b)[k],
-                    sems.at[len(runs) * (2 * s + b) + k],
-                )
-                copy.start()
-                copies.append(copy)
-    for copy in copies:
-        copy.wait()
+                kept[c] = result[2 * s + b, c] * scale
+            finished(s, b)
 
 
 def inner_kernel(
     edge_ref, middle_ref, far_middle_ref, ra_ref, dec_ref, box_ref, gather_ref,
-    out_ref, done_ref, edges_ref,
+    out_ref, last_ref, done_ref, edges_ref,
     source, smooth, result, framed, sems,
     *, batch,
 ):
@@ -410,26 +410,47 @@
                             source.at[part], j * ROWS + 32 * half + 16 * k, main,
                             (packed, packed), (64 * k, 64 * k + 32),
                         )
-                channels_at.append(8 * (i // 4) + 4 * half_z + i % 4)
+                channels_at.append((i, half_z))
             smooth_ra(source.at[part], ra_ref, ROWS, channels_at, done_ref, edges_ref)
-    beside = beside_squares([(dec_ref, edges_ref)], box_ref, gather_ref)
-
-    def targets(s, b):
-        return [out_ref.at[s, b, :, pl.ds(EDGE, ROWS - 2 * EDGE), :]]
-
-    snr_rows(
-        [(dec_ref, done_ref)], beside, (), inner_runs, targets, smooth, result, framed, sems
-    )
+    beside = functools.partial(beside_squares, [(dec_ref, edges_ref)], box_ref, gather_ref)
+
+    copies = []
+
+    def finished(s, b):
+        if s == 2:
+            return
+        rows = pl.ds(EDGE, ROWS - 2 * EDGE)
+        copy = pltpu.make_async_copy(
+            result.at[2 * s + b], out_ref.at[s, b, :, rows, :], sems.at[2 * s + b]
+        )
+        copy.start()
+        copies.append(copy)
+
+    parts = [(dec_ref, done_ref)]
+    snr_rows(parts, beside, (), inner_runs, smooth, result, framed, finished, last_ref)
+    for copy in copies:
+        copy.wait()
 
 
 def outer_kernel(
-    held_ref, chip_ref, next_ref, done_ref, edges_ref,
+    held_ref, last_ref, chip_ref, next_ref, done_ref, edges_ref,
     ra_ref, dec_ref, dec_halo_ref, box_ref, gather_ref,
     out_ref,
     source, halo_done, halo_edges, smooth, result, framed, sems,
     *, batch,
 ):
+    copies = []
+
+    def send(rows_ref, s, b, at):
+        copy = pltpu.make_async_copy(
+            rows_ref, out_ref.at[s, b, :, pl.ds(at, rows_ref.shape[1]), :], sems.at[len(copies)]
+        )
+        copy.start()
+        copies.append(copy)
+
     del held_ref
+    for b in range(2):
+        send(last_ref.at[b], 2, b, EDGE)
     channels = done_ref.shape[2] // LANES
     near = (lax.axis_index("ra") // 4) % 2
     dec_at, dec_n = lax.axis_index("dec"), lax.axis_size("dec")
@@ -448,19 +469,23 @@
                     (packed, packed), (lanes, lanes + 32),
                 )
             half_z = near if part == 0 else 1 - near
-            channels_at.append(8 * (i // 4) + 4 * half_z + i % 4)
+            channels_at.append((i, half_z))
         smooth_ra(source.at[step % 2], ra_ref, 2 * EDGE, channels_at, halo_done, halo_edges)
     dec_halo_ref = dec_halo_ref.at[dec_at % 2]
     parts = [(dec_ref, done_ref), (dec_halo_ref, halo_done)]
-    beside = beside_squares(
-        [(dec_ref, edges_ref), (dec_halo_ref, halo_edges)], box_ref, gather_ref
-    )
-
-    def targets(s, b):
-        return [out_ref.at[s, b, :, pl.ds(at, EDGE), :] for at in (0, ROWS - EDGE)]
+    beside = functools.partial(
+        beside_squares, [(dec_ref, edges_ref), (dec_halo_ref, halo_edges)], box_ref, gather_ref
+    )
+
+    def finished(s, b):
+        for k, (first, length, _, _) in enumerate(outer_runs):
+            rows_ref = result.at[2 * s + b, :, pl.ds(first, length), :]
+            send(rows_ref, s, b, (0, ROWS - EDGE)[k])
 
     outside = ((32, dec_at == 0), (35, dec_at == dec_n - 1))
-    snr_rows(parts, beside, outside, outer_runs, targets, smooth, result, framed, sems)
+    snr_rows(parts, beside, outside, outer_runs, smooth, result, framed, finished)
+    for copy in copies:
+        copy.wait()
 
 
 def local(cube):
@@ -506,15 +531,17 @@
 
     def regroup_edges(part, near_part, middle):
         chunks = call(edge_rows_kernel, chunk, (part, near_part), "edge_rows", (middle,))
-        chunks = regroup(chunks)
-        return (chunks, *call(edge_kernel, (edge, edge), (chunks,), "edges"))
+        return regroup(chunks)
 
     def no_edges(part, near_part, middle):
-        return jnp.zeros(chunk.shape, f32), jnp.zeros(edge.shape, f32), jnp.zeros(edge.shape, f32)
+        return jnp.zeros(chunk.shape, f32)
 
     edge = jax.ShapeDtypeStruct((channels * (EDGE + 4), LANES), f32)
-    edge_chunk, for_chip, for_next = lax.cond(
+    edge_chunk = lax.cond(
         lax.axis_index("ra") >= 0, regroup_edges, no_edges, part, near_part, middle
+    )
+    for_chip, for_next, edge_chunk = call(
+        edge_kernel, (edge, edge, chunk), (), "edges", (edge_chunk,), [pltpu.SemaphoreType.DMA]
     )
     count = lax.axis_size("dec")
     on_chip = [(i, i ^ 1) for i in range(count)]
@@ -526,24 +553,27 @@
     anywhere = pl.BlockSpec(memory_space=pl.ANY)
     out = jax.ShapeDtypeStruct((3, 2, channels, ROWS, LANES), f32)
     batch = 8
-    work = [
-        pltpu.VMEM((2, OUT, channels * LANES), f32),
-        pltpu.VMEM((6, channels, 2 * EDGE, LANES), f32),
-        pltpu.VMEM((2, ROWS + 16, LANES), f32),
-    ]
+    smooth = pltpu.VMEM((2, OUT, channels * LANES), f32)
+    framed = pltpu.VMEM((2, ROWS + 16, LANES), f32)
+    result = (6, channels, 2 * EDGE, LANES)
     params = pltpu.CompilerParams(vmem_limit_bytes=32 * 2**20)
-    held, done, edges = pl.pallas_call(
+    held, last, done, edges = pl.pallas_call(
         functools.partial(inner_kernel, batch=batch),
         out_shape=(
             out,
+            jax.ShapeDtypeStruct((2, *result[1:]), f32),
             jax.ShapeDtypeStruct((3, 2 * ROWS, channels * LANES), jnp.bfloat16),
             jax.ShapeDtypeStruct((2, ROWS, LANES), f32),
         ),
         in_specs=[vmem] * 7,
-        out_specs=(anywhere, vmem, vmem),
-        scratch_shapes=[pltpu.VMEM((2, batch * ROWS, 3 * LANES), jnp.bfloat16)]
-        + work
-        + [pltpu.SemaphoreType.DMA((6,))],
+        out_specs=(anywhere, vmem, vmem, vmem),
+        scratch_shapes=[
+            pltpu.VMEM((2, batch * ROWS, 3 * LANES), jnp.bfloat16),
+            smooth,
+            pltpu.VMEM(result, f32),
+            framed,
+            pltpu.SemaphoreType.DMA((4,)),
+        ],
         compiler_params=params,
         cost_estimate=pl.CostEstimate(
             flops=2 * 10**9, bytes_accessed=8 * 2**20, transcendentals=0
@@ -560,15 +590,17 @@
     return pl.pallas_call(
         functools.partial(outer_kernel, batch=batch),
         out_shape=out,
-        in_specs=[anywhere] + [vmem] * 9,
+        in_specs=[anywhere] + [vmem] * 10,
         out_specs=anywhere,
         scratch_shapes=[
             pltpu.VMEM((2, batch * 2 * EDGE, 3 * LANES), jnp.bfloat16),
             pltpu.VMEM((3, 4 * EDGE, channels * LANES), jnp.bfloat16),
             pltpu.VMEM((2, 2 * EDGE, LANES), f32),
-        ]
-        + work
-        + [pltpu.SemaphoreType.DMA((12,))],
+            smooth,
+            pltpu.VMEM(result, f32),
+            framed,
+            pltpu.SemaphoreType.DMA((14,)),
+        ],
         input_output_aliases={0: 0},
         compiler_params=params,
         cost_estimate=pl.CostEstimate(
@@ -576,7 +608,7 @@
         ),
         name="outer",
     )(
-        held, from_chip, from_next, done, edges, along,
+        held, last, from_chip, from_next, done, edges, along,
         jnp.asarray(dec_weights(outer_out, tile_rows)),
         jnp.asarray(halo_weights), box, gather,
     )

time: 60.6 us -> 59.3 us (0.979)
  Pallas kernels: 14.1 us -> 11.6 us
  waiting for transfers between devices: 0.01 us -> 1.57 us
    pallas_call x1, Pallas kernels: 5.77 us -> 4.2 us  [local(): pl.pallas_call(functools.partial(inner_kernel, batch=batch), out_shape=(o...]
    ppermute x1, waiting for transfers between devices: 0.01 us -> 1.56 us  [local(): from_next = lax.ppermute(for_next, 'dec', beyond)]
    pallas_call x4, Pallas kernels: 4.13 us -> 3.26 us  [call(): pl.pallas_call(kernel, out_shape=shapes, in_specs=[pl.BlockSpec(memory_sp...]
  transfers between devices with their start and end apart: 4 -> 4, of which waited for: 0 -> 1; matrix products, arithmetic and copies ran while one was open for 0% -> 0% of each run, Pallas kernels for 14% -> 10%
where the time goes in v3:
time: 59.3 us; the launch traced here: 59.1 us
  blocking collectives  31 us (52%)
  starting transfers between devices  14.8 us (25%)
  Pallas kernels  11.6 us (20%)
  waiting for transfers between devices  1.57 us (3%)
    all_to_all x2, blocking collectives, regroup(): lax.all_to_all(chunks, 'ra', split_axis=0, concat_axis=0, tiled=True, axi...  31 us
    ppermute x1, starting transfers between devices, local(): part = lax.ppermute(part, 'ra', across)  7.83 us
    pallas_call x1, Pallas kernels, local(): pl.pallas_call(functools.partial(inner_kernel, batch=batch), out_shape=(o...  4.2 us
    pallas_call x1, Pallas kernels, local(): pl.pallas_call(functools.partial(outer_kernel, batch=batch), out_shape=ou...  4.12 us
    ppermute x1, starting transfers between devices, local(): from_chip = lax.ppermute(for_chip, 'dec', on_chip)  3.73 us
    pallas_call x4, Pallas kernels, call(): pl.pallas_call(kernel, out_shape=shapes, in_specs=[pl.BlockSpec(memory_sp...  3.26 us
    ppermute x1, starting transfers between devices, local(): from_next = lax.ppermute(for_next, 'dec', beyond)  2.55 us
    ppermute x1, waiting for transfers between devices, local(): from_next = lax.ppermute(for_next, 'dec', beyond)  1.56 us
  transfers between devices with their start and end apart: 4, of which 1 were waited for; matrix products, arithmetic and copies ran while one was open for 0% of the time, Pallas kernels for 10%

profile of v3, /device:TPU:1, one launch (start us, length us, event | category | flops | bytes accessed | tf_op | source)
XLA Modules:
  0.0 59.1 jit_solution(10357349915129846098)
XLA Ops:
  0.0 0.0 copy-start
  0.0 0.0 copy-start.2
  0.0 0.0 copy-start.1
  0.0 0.0 copy-start.5
  0.0 1.3 %columns.1 = (f32[17,32,128]{2,1,0:T(8,128)S(1)}, f32[17,32,128]{2,1,0:T(8,128)S(1)}) custom-call(f32[1,64,4096]{2,1,0:T(8,128)} %cube_ref.2), custom_call_target="tpu_custom_call" | custom-call | tf_op jit(solution)/shard_map/columns/pallas_call | solution.py:497
  1.3 7.8 %collective-permute-start = (f32[17,32,128]{2,1,0:T(8,128)S(1)}, f32[17,32,128]{2,1,0:T(8,128)S(1)}, u32[]{:S(2)}, u32[]{:S(2)}) collective-permute-start(f32[17,32,128]{2,1,0:T(8,128)S(1)} %get-tuple-element.30), channel_id=1, source_target_pairs={{0,32},{8,40},{16,48},{24,56},{32,0},{40,8},{48,16},{56,24},{64,96... | collective-permute-start | bytes 835592 | tf_op jit(solution)/shard_map/ppermute | solution.py:520
  9.2 18.9 %conditional.2 = (f32[16,80,128]{2,1,0:T(8,128)S(1)}) conditional(s32[]{:T(128)} %convert_element_type.4, () %tuple.18, f32[1,64,4096]{2,1,0:T(8,128)} %cube_ref.2), branch_computations={%region_0.0_spmd, %region_1.0_spmd} | conditional | bytes 1310728 | solution.py:529
  9.2 1.3 %middle.1 = f32[16,80,128]{2,1,0:T(8,128)S(1)} custom-call(f32[1,64,4096]{2,1,0:T(8,128)} %cube_ref.1), custom_call_target="tpu_custom_call" | custom-call | tf_op jit(solution)/shard_map/cond/branch_1_fun/middle/pallas_call | solution.py:497
  10.5 17.6 %all_to_all.8 = f32[16,80,128]{2,1,0:T(8,128)S(1)} all-to-all(f32[16,80,128]{2,1,0:T(8,128)S(1)} %middle.1), channel_id=1, replica_groups={{0,8,16,24,64,72,80,88,128,136,144,152,192,200,208,216},{32,40,48,56,96..., dimensions={0} | all-to-all | bytes 1310720 | tf_op jit(solution)/shard_map/cond/branch_1_fun/all_to_all | solution.py:511
  28.1 0.0 copy-start.3
  28.1 0.0 copy-start.4
  28.1 0.7 %collective-permute-start.1 = (f32[16,40,128]{2,1,0:T(8,128)S(1)}, f32[16,40,128]{2,1,0:T(8,128)S(1)}, u32[]{:S(2)}, u32[]{:S(2)}) collective-permute-start(f32[16,40,128]{2,1,0:T(8,128)S(1)} %slice.4), channel_id=1, source_target_pairs={{0,32},{8,40},{16,48},{24,56},{32,0},{40,8},{48,16},{56,24},{64,96... | collective-permute-start | bytes 983048 | tf_op jit(solution)/shard_map/ppermute | solution.py:530
  28.8 0.0 collective-permute-done
  28.8 13.7 %conditional.3 = (f32[16,80,128]{2,1,0:T(8,128)S(1)}) conditional(s32[]{:T(128)} %convert_element_type.4, () %tuple.17, (f32[16,80,128]{2,1,0:T(8,128)S(1)}, f32[17,32,128]{2,1,0:T(8,128)S(1)}, f32[17,32,128]{2,1,0:T(8,128)S(1)}) %tuple.19), branch_computations={%region_2.0_spmd, %region_3.0_spmd} | conditional | bytes 1310728 | solution.py:540
  28.8 0.3 edge_rows.1
  29.1 13.4 %all_to_all.9 = f32[16,80,128]{2,1,0:T(8,128)S(1)} all-to-all(f32[16,80,128]{2,1,0:T(8,128)S(1)} %edge_rows.1), channel_id=1, replica_groups={{0,8,16,24,64,72,80,88,128,136,144,152,192,200,208,216},{32,40,48,56,96..., dimensions={0} | all-to-all | bytes 1310720 | tf_op jit(solution)/shard_map/cond/branch_1_fun/all_to_all | solution.py:511
  42.5 0.4 edges.1
  42.9 3.7 %collective-permute-start.2 = (f32[640,128]{1,0:T(8,128)S(1)}, f32[640,128]{1,0:T(8,128)S(1)}, u32[]{:S(2)}, u32[]{:S(2)}) collective-permute-start(f32[640,128]{1,0:T(8,128)S(1)} %get-tuple-element.35), channel_id=1, source_target_pairs={{0,1},{1,0},{2,3},{3,2},{4,5},{5,4},{6,7},{7,6},{8,9},{9,8},{10,11... | collective-permute-start | bytes 983048 | tf_op jit(solution)/shard_map/ppermute | solution.py:549
  46.6 2.5 %collective-permute-start.3 = (f32[640,128]{1,0:T(8,128)S(1)}, f32[640,128]{1,0:T(8,128)S(1)}, u32[]{:S(2)}, u32[]{:S(2)}) collective-permute-start(f32[640,128]{1,0:T(8,128)S(1)} %get-tuple-element.36), channel_id=1, source_target_pairs={{1,2},{3,4},{5,6},{2,1},{4,3},{6,5},{9,10},{11,12},{13,14},{10,9},... | collective-permute-start | bytes 983048 | tf_op jit(solution)/shard_map/ppermute | solution.py:550
  49.2 0.0 collective-permute-done.1.far_middle_ref
  49.2 0.0 copy-done
  49.2 0.0 copy-done.2
  49.2 0.0 copy-done.1
  49.2 0.0 copy-done.5
  49.2 4.2 %inner.1 = (f32[3,2,32,64,128]{4,3,2,1,0:T(8,128)}, f32[2,32,32,128]{3,2,1,0:T(8,128)S(1)}, bf16[3,128,4096]{2,1,0:T(8,128)(2,1)S(1)}, f32[2,64,128]{2,1,0:T(8,128)S(1)}) custom-call(f32[16,80,128]{2,1,0:T(8,128)S(1)} %get-tuple-element.32.edge_ref, f32[16,80,128]{2,1,0:T(8,128)S(1)} %get-tuple-element.39.middle_ref, ...), custom_call_target="tpu_custom_call" | custom-call | flops 2000000000 | bytes 8388608 | tf_op jit(solution)/shard_map/inner/pallas_call | solution.py:560
  53.4 0.0 collective-permute-done.2.chip_ref
  53.5 1.6 %collective-permute-done.3.next_ref = f32[640,128]{1,0:T(8,128)S(1)} collective-permute-done((f32[640,128]{1,0:T(8,128)S(1)}, f32[640,128]{1,0:T(8,128)S(1)}, u32[]{:S(2)}, u32[]{:S(2)}) %collective-permute-start.3) | collective-permute-done | bytes 327712 | tf_op jit(solution)/shard_map/ppermute | solution.py:550
  55.0 0.0 copy-done.3
  55.0 0.0 copy-done.4
  55.0 4.1 %outer.1 = f32[3,2,32,64,128]{4,3,2,1,0:T(8,128)} custom-call(f32[3,2,32,64,128]{4,3,2,1,0:T(8,128)} %get-tuple-element.33.held_ref, f32[2,32,32,128]{3,2,1,0:T(8,128)S(1)} %get-tuple-element.34.last_ref, f32[640,128]{1,0:T(8,128)S(1)} %collective-permute-done.2.chip_ref, ...), custom_call_target="tpu_custom_call", output_to_operand_aliasing={{}: (0, {})} | custom-call | flops 1000000000 | bytes 8388608 | tf_op jit(solution)/shard_map/outer/pallas_call | solution.py:590
  (1 shorter events, 0.0 us)
Async XLA Ops:
  0.0 49.2 %copy-start = (bf16[512,512]{1,0:T(8,128)(2,1)S(1)}, bf16[512,512]{1,0:T(8,128)(2,1)}, u32[]{:S(2)}) copy-start(bf16[512,512]{1,0:T(8,128)(2,1)} %constant.26.clone.ra_ref) | copy-start | bytes 1572868
  0.0 49.2 %copy-start.2 = (bf16[256,384]{1,0:T(8,128)(2,1)S(1)}, bf16[256,384]{1,0:T(8,128)(2,1)}, u32[]{:S(2)}) copy-start(bf16[256,384]{1,0:T(8,128)(2,1)} %constant.25.clone.gather_ref) | copy-start | bytes 589828
  0.0 49.2 %copy-start.1 = (bf16[256,512]{1,0:T(8,128)(2,1)S(1)}, bf16[256,512]{1,0:T(8,128)(2,1)}, u32[]{:S(2)}) copy-start(bf16[256,512]{1,0:T(8,128)(2,1)} %constant.24.clone.box_ref) | copy-start | bytes 786436
  0.0 49.2 %copy-start.5 = (bf16[3,80,128]{2,1,0:T(8,128)(2,1)S(1)}, bf16[3,80,128]{2,1,0:T(8,128)(2,1)}, u32[]{:S(2)}) copy-start(bf16[3,80,128]{2,1,0:T(8,128)(2,1)} %constant.27.clone.dec_ref) | copy-start | bytes 184324
  1.3 27.5 %collective-permute-start = (f32[17,32,128]{2,1,0:T(8,128)S(1)}, f32[17,32,128]{2,1,0:T(8,128)S(1)}, u32[]{:S(2)}, u32[]{:S(2)}) collective-permute-start(f32[17,32,128]{2,1,0:T(8,128)S(1)} %get-tuple-element.30), channel_id=1, source_target_pairs={{0,32},{8,40},{16,48},{24,56},{32,0},{40,8},{48,16},{56,24},{64,96... | collective-permute-start | bytes 835592 | tf_op jit(solution)/shard_map/ppermute | solution.py:520
  28.1 26.9 %copy-start.3 = (bf16[2,3,80,64]{3,2,1,0:T(8,128)(2,1)S(1)}, bf16[2,3,80,64]{3,2,1,0:T(8,128)(2,1)}, u32[]{:S(2)}) copy-start(bf16[2,3,80,64]{3,2,1,0:T(8,128)(2,1)} %constant.29.clone.dec_halo_ref) | copy-start | bytes 184324
  28.1 26.9 %copy-start.4 = (bf16[3,80,128]{2,1,0:T(8,128)(2,1)S(1)}, bf16[3,80,128]{2,1,0:T(8,128)(2,1)}, u32[]{:S(2)}) copy-start(bf16[3,80,128]{2,1,0:T(8,128)(2,1)} %constant.28.clone.dec_ref) | copy-start | bytes 184324
  28.1 21.1 %collective-permute-start.1 = (f32[16,40,128]{2,1,0:T(8,128)S(1)}, f32[16,40,128]{2,1,0:T(8,128)S(1)}, u32[]{:S(2)}, u32[]{:S(2)}) collective-permute-start(f32[16,40,128]{2,1,0:T(8,128)S(1)} %slice.4), channel_id=1, source_target_pairs={{0,32},{8,40},{16,48},{24,56},{32,0},{40,8},{48,16},{56,24},{64,96... | collective-permute-start | bytes 983048 | tf_op jit(solution)/shard_map/ppermute | solution.py:530
  42.9 10.6 %collective-permute-start.2 = (f32[640,128]{1,0:T(8,128)S(1)}, f32[640,128]{1,0:T(8,128)S(1)}, u32[]{:S(2)}, u32[]{:S(2)}) collective-permute-start(f32[640,128]{1,0:T(8,128)S(1)} %get-tuple-element.35), channel_id=1, source_target_pairs={{0,1},{1,0},{2,3},{3,2},{4,5},{5,4},{6,7},{7,6},{8,9},{9,8},{10,11... | collective-permute-start | bytes 983048 | tf_op jit(solution)/shard_map/ppermute | solution.py:549
  46.6 8.4 %collective-permute-start.3 = (f32[640,128]{1,0:T(8,128)S(1)}, f32[640,128]{1,0:T(8,128)S(1)}, u32[]{:S(2)}, u32[]{:S(2)}) collective-permute-start(f32[640,128]{1,0:T(8,128)S(1)} %get-tuple-element.36), channel_id=1, source_target_pairs={{1,2},{3,4},{5,6},{2,1},{4,3},{6,5},{9,10},{11,12},{13,14},{10,9},... | collective-permute-start | bytes 983048 | tf_op jit(solution)/shard_map/ppermute | solution.py:550

commit v4 on v3

--- a/solution.py
+++ b/solution.py
@@ -23,7 +23,10 @@
 edge_rows = tuple(range(0, EDGE)) + tuple(range(ROWS - EDGE, ROWS))
 middle_rows = tuple(range(EDGE, ROWS - EDGE))
 tile_rows = edge_rows + middle_rows
-above_rows, below_rows = tuple(range(-EDGE, 0)), tuple(range(ROWS, ROWS + EDGE))
+NEED = 3 * max(sigma_values) + 1
+far_away = (1000,) * (EDGE - NEED)
+above_rows = tuple(range(-NEED, 0)) + far_away
+below_rows = tuple(range(ROWS, ROWS + NEED)) + far_away
 inner_out = middle_rows + (EDGE - 1, ROWS - EDGE)
 outer_out = edge_rows + (-1, EDGE, ROWS - EDGE - 1, ROWS)
 inner_runs = ((0, 32, 32, 33),)
@@ -240,18 +243,25 @@
     count = edge_ref.shape[0]
     channels = 2 * count
     lane = lane_index((8, LANES))
+    row = lax.broadcasted_iota(jnp.int32, (8, LANES), 0)
     for ref, lower in ((chip_ref, 1 - odd), (next_ref, odd)):
-        rows = pl.multiple_of(EDGE * lower, EDGE)
         for part, start in enumerate((HALF, 0)):
             for i in range(count):
-                at = (part * count + i) * EDGE
-                ref[at : at + EDGE, :] = edge_ref[i, pl.ds(start + rows, EDGE), :]
+                at = (part * count + i) * NEED
+                upper_rows = edge_ref[i, start : start + NEED, :]
+                lower_rows = edge_ref[i, start + 2 * EDGE - NEED : start + 2 * EDGE, :]
+                ref[at : at + NEED, :] = jnp.where(lower == 1, lower_rows, upper_rows)
             for pair in range(count // 2):
-                at = channels * EDGE + 8 * (part * count // 2 + pair)
+                at = channels * NEED + 8 * (part * count // 2 + pair)
                 first = edge_ref[2 * pair, start + 32 : start + HALF, :]
                 second = edge_ref[2 * pair + 1, start + 32 : start + HALF, :]
                 upper_halves = jnp.where(lane < 64, first, pltpu.roll(second, 64, 1))
                 lower_halves = jnp.where(lane < 64, pltpu.roll(first, 64, 1), second)
+                lower_halves = pltpu.roll(lower_halves, 8 - (EDGE - NEED), 0)
+                follows = (row >= 8 - (EDGE - NEED)) & (lane // 32 % 2 == 0)
+                lower_halves = jnp.where(
+                    follows, pltpu.roll(lower_halves, LANES - 32, 1), lower_halves
+                )
                 ref[at : at + 8, :] = jnp.where(lower == 1, lower_halves, upper_halves)
 
 
@@ -461,11 +471,11 @@
             at = step * batch + j
             part, i = at // (channels // 2), at % (channels // 2)
             for k, ref in enumerate((chip_ref, next_ref)):
-                row = channels * EDGE + 8 * (at // 2)
+                row = channels * NEED + 8 * (at // 2)
                 packed = ref[row : row + 8, :]
                 lanes = 64 * (at % 2)
                 put_rows(
-                    source.at[step % 2], 2 * EDGE * j + EDGE * k, ref[at * EDGE : (at + 1) * EDGE, :],
+                    source.at[step % 2], 2 * EDGE * j + EDGE * k, ref[at * NEED : at * NEED + EDGE, :],
                     (packed, packed), (lanes, lanes + 32),
                 )
             half_z = near if part == 0 else 1 - near
@@ -536,7 +546,7 @@
     def no_edges(part, near_part, middle):
         return jnp.zeros(chunk.shape, f32)
 
-    edge = jax.ShapeDtypeStruct((channels * (EDGE + 4), LANES), f32)
+    edge = jax.ShapeDtypeStruct((channels * (NEED + 4), LANES), f32)
     edge_chunk = lax.cond(
         lax.axis_index("ra") >= 0, regroup_edges, no_edges, part, near_part, middle
     )

time: 59.3 us -> 58.9 us (level)
  transfers between devices with their start and end apart: 4 -> 4, of which waited for: 1 -> 1; matrix products, arithmetic and copies ran while one was open for 0% -> 0% of each run, Pallas kernels for 10% -> 11%
where the time goes in v4:
time: 58.9 us; the launch traced here: 58.7 us
  blocking collectives  31 us (53%)
  starting transfers between devices  14.8 us (25%)
  Pallas kernels  11.6 us (20%)
  waiting for transfers between devices  1.05 us (2%)
    all_to_all x2, blocking collectives, regroup(): lax.all_to_all(chunks, 'ra', split_axis=0, concat_axis=0, tiled=True, axi...  31 us
    ppermute x1, starting transfers between devices, local(): part = lax.ppermute(part, 'ra', across)  7.83 us
    pallas_call x1, Pallas kernels, local(): pl.pallas_call(functools.partial(inner_kernel, batch=batch), out_shape=(o...  4.19 us
    pallas_call x1, Pallas kernels, local(): pl.pallas_call(functools.partial(outer_kernel, batch=batch), out_shape=ou...  4.11 us
    ppermute x1, starting transfers between devices, local(): from_chip = lax.ppermute(for_chip, 'dec', on_chip)  3.73 us
    pallas_call x4, Pallas kernels, call(): pl.pallas_call(kernel, out_shape=shapes, in_specs=[pl.BlockSpec(memory_sp...  3.33 us
    ppermute x1, starting transfers between devices, local(): from_next = lax.ppermute(for_next, 'dec', beyond)  2.55 us
  transfers between devices with their start and end apart: 4, of which 1 were waited for; matrix products, arithmetic and copies ran while one was open for 0% of the time, Pallas kernels for 11%

profile of v4, /device:TPU:1, one launch (start us, length us, event | category | flops | bytes accessed | tf_op | source)
XLA Modules:
  0.0 58.7 jit_solution(12756683486390703393)
XLA Ops:
  0.0 0.0 copy-start
  0.0 0.0 copy-start.2
  0.0 0.0 copy-start.1
  0.0 0.0 copy-start.5
  0.0 1.3 %columns.1 = (f32[17,32,128]{2,1,0:T(8,128)S(1)}, f32[17,32,128]{2,1,0:T(8,128)S(1)}) custom-call(f32[1,64,4096]{2,1,0:T(8,128)} %cube_ref.2), custom_call_target="tpu_custom_call" | custom-call | tf_op jit(solution)/shard_map/columns/pallas_call | solution.py:507
  1.3 7.8 %collective-permute-start = (f32[17,32,128]{2,1,0:T(8,128)S(1)}, f32[17,32,128]{2,1,0:T(8,128)S(1)}, u32[]{:S(2)}, u32[]{:S(2)}) collective-permute-start(f32[17,32,128]{2,1,0:T(8,128)S(1)} %get-tuple-element.30), channel_id=1, source_target_pairs={{0,32},{8,40},{16,48},{24,56},{32,0},{40,8},{48,16},{56,24},{64,96... | collective-permute-start | bytes 835592 | tf_op jit(solution)/shard_map/ppermute | solution.py:530
  9.2 18.9 %conditional.2 = (f32[16,80,128]{2,1,0:T(8,128)S(1)}) conditional(s32[]{:T(128)} %convert_element_type.4, () %tuple.18, f32[1,64,4096]{2,1,0:T(8,128)} %cube_ref.2), branch_computations={%region_0.0_spmd, %region_1.0_spmd} | conditional | bytes 1310728 | solution.py:539
  9.2 1.3 %middle.1 = f32[16,80,128]{2,1,0:T(8,128)S(1)} custom-call(f32[1,64,4096]{2,1,0:T(8,128)} %cube_ref.1), custom_call_target="tpu_custom_call" | custom-call | tf_op jit(solution)/shard_map/cond/branch_1_fun/middle/pallas_call | solution.py:507
  10.5 17.6 %all_to_all.8 = f32[16,80,128]{2,1,0:T(8,128)S(1)} all-to-all(f32[16,80,128]{2,1,0:T(8,128)S(1)} %middle.1), channel_id=1, replica_groups={{0,8,16,24,64,72,80,88,128,136,144,152,192,200,208,216},{32,40,48,56,96..., dimensions={0} | all-to-all | bytes 1310720 | tf_op jit(solution)/shard_map/cond/branch_1_fun/all_to_all | solution.py:521
  28.1 0.0 copy-start.3
  28.1 0.0 copy-start.4
  28.1 0.7 %collective-permute-start.1 = (f32[16,40,128]{2,1,0:T(8,128)S(1)}, f32[16,40,128]{2,1,0:T(8,128)S(1)}, u32[]{:S(2)}, u32[]{:S(2)}) collective-permute-start(f32[16,40,128]{2,1,0:T(8,128)S(1)} %slice.4), channel_id=1, source_target_pairs={{0,32},{8,40},{16,48},{24,56},{32,0},{40,8},{48,16},{56,24},{64,96... | collective-permute-start | bytes 983048 | tf_op jit(solution)/shard_map/ppermute | solution.py:540
  28.8 0.0 collective-permute-done
  28.8 13.7 %conditional.3 = (f32[16,80,128]{2,1,0:T(8,128)S(1)}) conditional(s32[]{:T(128)} %convert_element_type.4, () %tuple.17, (f32[16,80,128]{2,1,0:T(8,128)S(1)}, f32[17,32,128]{2,1,0:T(8,128)S(1)}, f32[17,32,128]{2,1,0:T(8,128)S(1)}) %tuple.19), branch_computations={%region_2.0_spmd, %region_3.0_spmd} | conditional | bytes 1310728 | solution.py:550
  28.8 0.3 edge_rows.1
  29.1 13.4 %all_to_all.9 = f32[16,80,128]{2,1,0:T(8,128)S(1)} all-to-all(f32[16,80,128]{2,1,0:T(8,128)S(1)} %edge_rows.1), channel_id=1, replica_groups={{0,8,16,24,64,72,80,88,128,136,144,152,192,200,208,216},{32,40,48,56,96..., dimensions={0} | all-to-all | bytes 1310720 | tf_op jit(solution)/shard_map/cond/branch_1_fun/all_to_all | solution.py:521
  42.5 0.4 edges.1
  43.0 3.7 %collective-permute-start.2 = (f32[544,128]{1,0:T(8,128)S(1)}, f32[544,128]{1,0:T(8,128)S(1)}, u32[]{:S(2)}, u32[]{:S(2)}) collective-permute-start(f32[544,128]{1,0:T(8,128)S(1)} %get-tuple-element.35), channel_id=1, source_target_pairs={{0,1},{1,0},{2,3},{3,2},{4,5},{5,4},{6,7},{7,6},{8,9},{9,8},{10,11... | collective-permute-start | bytes 835592 | tf_op jit(solution)/shard_map/ppermute | solution.py:559
  46.7 2.5 %collective-permute-start.3 = (f32[544,128]{1,0:T(8,128)S(1)}, f32[544,128]{1,0:T(8,128)S(1)}, u32[]{:S(2)}, u32[]{:S(2)}) collective-permute-start(f32[544,128]{1,0:T(8,128)S(1)} %get-tuple-element.36), channel_id=1, source_target_pairs={{1,2},{3,4},{5,6},{2,1},{4,3},{6,5},{9,10},{11,12},{13,14},{10,9},... | collective-permute-start | bytes 835592 | tf_op jit(solution)/shard_map/ppermute | solution.py:560
  49.2 0.0 collective-permute-done.1.far_middle_ref
  49.3 0.0 copy-done
  49.3 0.0 copy-done.2
  49.3 0.0 copy-done.1
  49.3 0.0 copy-done.5
  49.3 4.2 %inner.1 = (f32[3,2,32,64,128]{4,3,2,1,0:T(8,128)}, f32[2,32,32,128]{3,2,1,0:T(8,128)S(1)}, bf16[3,128,4096]{2,1,0:T(8,128)(2,1)S(1)}, f32[2,64,128]{2,1,0:T(8,128)S(1)}) custom-call(f32[16,80,128]{2,1,0:T(8,128)S(1)} %get-tuple-element.32.edge_ref, f32[16,80,128]{2,1,0:T(8,128)S(1)} %get-tuple-element.39.middle_ref, ...), custom_call_target="tpu_custom_call" | custom-call | flops 2000000000 | bytes 8388608 | tf_op jit(solution)/shard_map/inner/pallas_call | solution.py:570
  53.5 0.0 collective-permute-done.2.chip_ref
  53.5 1.0 %collective-permute-done.3.next_ref = f32[544,128]{1,0:T(8,128)S(1)} collective-permute-done((f32[544,128]{1,0:T(8,128)S(1)}, f32[544,128]{1,0:T(8,128)S(1)}, u32[]{:S(2)}, u32[]{:S(2)}) %collective-permute-start.3) | collective-permute-done | bytes 278560 | tf_op jit(solution)/shard_map/ppermute | solution.py:560
  54.6 0.0 copy-done.3
  54.6 0.0 copy-done.4
  54.6 4.1 %outer.1 = f32[3,2,32,64,128]{4,3,2,1,0:T(8,128)} custom-call(f32[3,2,32,64,128]{4,3,2,1,0:T(8,128)} %get-tuple-element.33.held_ref, f32[2,32,32,128]{3,2,1,0:T(8,128)S(1)} %get-tuple-element.34.last_ref, f32[544,128]{1,0:T(8,128)S(1)} %collective-permute-done.2.chip_ref, ...), custom_call_target="tpu_custom_call", output_to_operand_aliasing={{}: (0, {})} | custom-call | flops 1000000000 | bytes 8388608 | tf_op jit(solution)/shard_map/outer/pallas_call | solution.py:600
  (1 shorter events, 0.0 us)
Async XLA Ops:
  0.0 49.3 %copy-start = (bf16[512,512]{1,0:T(8,128)(2,1)S(1)}, bf16[512,512]{1,0:T(8,128)(2,1)}, u32[]{:S(2)}) copy-start(bf16[512,512]{1,0:T(8,128)(2,1)} %constant.26.clone.ra_ref) | copy-start | bytes 1572868
  0.0 49.3 %copy-start.2 = (bf16[256,384]{1,0:T(8,128)(2,1)S(1)}, bf16[256,384]{1,0:T(8,128)(2,1)}, u32[]{:S(2)}) copy-start(bf16[256,384]{1,0:T(8,128)(2,1)} %constant.25.clone.gather_ref) | copy-start | bytes 589828
  0.0 49.3 %copy-start.1 = (bf16[256,512]{1,0:T(8,128)(2,1)S(1)}, bf16[256,512]{1,0:T(8,128)(2,1)}, u32[]{:S(2)}) copy-start(bf16[256,512]{1,0:T(8,128)(2,1)} %constant.24.clone.box_ref) | copy-start | bytes 786436
  0.0 49.3 %copy-start.5 = (bf16[3,80,128]{2,1,0:T(8,128)(2,1)S(1)}, bf16[3,80,128]{2,1,0:T(8,128)(2,1)}, u32[]{:S(2)}) copy-start(bf16[3,80,128]{2,1,0:T(8,128)(2,1)} %constant.27.clone.dec_ref) | copy-start | bytes 184324
  1.3 27.5 %collective-permute-start = (f32[17,32,128]{2,1,0:T(8,128)S(1)}, f32[17,32,128]{2,1,0:T(8,128)S(1)}, u32[]{:S(2)}, u32[]{:S(2)}) collective-permute-start(f32[17,32,128]{2,1,0:T(8,128)S(1)} %get-tuple-element.30), channel_id=1, source_target_pairs={{0,32},{8,40},{16,48},{24,56},{32,0},{40,8},{48,16},{56,24},{64,96... | collective-permute-start | bytes 835592 | tf_op jit(solution)/shard_map/ppermute | solution.py:530
  28.1 26.5 %copy-start.3 = (bf16[2,3,80,64]{3,2,1,0:T(8,128)(2,1)S(1)}, bf16[2,3,80,64]{3,2,1,0:T(8,128)(2,1)}, u32[]{:S(2)}) copy-start(bf16[2,3,80,64]{3,2,1,0:T(8,128)(2,1)} %constant.29.clone.dec_halo_ref) | copy-start | bytes 184324
  28.1 26.5 %copy-start.4 = (bf16[3,80,128]{2,1,0:T(8,128)(2,1)S(1)}, bf16[3,80,128]{2,1,0:T(8,128)(2,1)}, u32[]{:S(2)}) copy-start(bf16[3,80,128]{2,1,0:T(8,128)(2,1)} %constant.28.clone.dec_ref) | copy-start | bytes 184324
  28.1 21.1 %collective-permute-start.1 = (f32[16,40,128]{2,1,0:T(8,128)S(1)}, f32[16,40,128]{2,1,0:T(8,128)S(1)}, u32[]{:S(2)}, u32[]{:S(2)}) collective-permute-start(f32[16,40,128]{2,1,0:T(8,128)S(1)} %slice.4), channel_id=1, source_target_pairs={{0,32},{8,40},{16,48},{24,56},{32,0},{40,8},{48,16},{56,24},{64,96... | collective-permute-start | bytes 983048 | tf_op jit(solution)/shard_map/ppermute | solution.py:540
  43.0 10.5 %collective-permute-start.2 = (f32[544,128]{1,0:T(8,128)S(1)}, f32[544,128]{1,0:T(8,128)S(1)}, u32[]{:S(2)}, u32[]{:S(2)}) collective-permute-start(f32[544,128]{1,0:T(8,128)S(1)} %get-tuple-element.35), channel_id=1, source_target_pairs={{0,1},{1,0},{2,3},{3,2},{4,5},{5,4},{6,7},{7,6},{8,9},{9,8},{10,11... | collective-permute-start | bytes 835592 | tf_op jit(solution)/shard_map/ppermute | solution.py:559
  46.7 7.9 %collective-permute-start.3 = (f32[544,128]{1,0:T(8,128)S(1)}, f32[544,128]{1,0:T(8,128)S(1)}, u32[]{:S(2)}, u32[]{:S(2)}) collective-permute-start(f32[544,128]{1,0:T(8,128)S(1)} %get-tuple-element.36), channel_id=1, source_target_pairs={{1,2},{3,4},{5,6},{2,1},{4,3},{6,5},{9,10},{11,12},{13,14},{10,9},... | collective-permute-start | bytes 835592 | tf_op jit(solution)/shard_map/ppermute | solution.py:560
